TPU v7x, 32 devices: a whole 2x2x4 slice. The times are simulated.
32 devices in a mesh: section: 4 (over y, core), row: 8 (over z, x).
Axes of the slice: x: 2, y: 2, z: 4, core: 2. Of those that a mesh axis runs over, the one named last changes fastest.
Arguments:
- coupling: bfloat16 [512, 128, 128], P(('section', 'row')), may hold values from -4 to 4
- diag_inverse: float32 [512, 128, 128], P(('section', 'row')), may hold values from -0.046875 to 0.046875
- pivot_inverse: bfloat16 [128, 128, 128], P(('section', 'row')), may hold values from -0.5 to 0.5
- cross_left: bfloat16 [4096, 128, 128], P(('section', 'row')), may hold values from -0.5 to 0.5
- cross_right: bfloat16 [4096, 128, 128], P(('section', 'row')), may hold values from -4 to 4
- cross_pivot: int32 [4096], P(('section', 'row')), may hold values from 0 to 3
- cross_owner: int32 [4096, 1], P(('section', 'row')), may hold values from 0 to 7; in each aligned block of 128 rows (0 to 127, 128 to 255, ...) at most 16 rows name the same one
- foreign_target_row: int32 [4096], P(('section', 'row')), may hold values from 0 to 15
- cross_count: int32 [32], P(('section', 'row')), may hold values from 1 to 128, 3072 in all
- local_left: bfloat16 [4096, 128, 128], P(('section', 'row')), may hold values from -0.5 to 0.5
- local_right: bfloat16 [4096, 128, 128], P(('section', 'row')), may hold values from -4 to 4
- local_pivot: int32 [4096], P(('section', 'row')), may hold values from 0 to 3
- local_target: int32 [4096], P(('section', 'row')), may hold values from 0 to 15
- adjoint_seed: float32 [512, 128, 128], P(('section', 'row')), may hold values from -48 to 48
Outputs:
- coupling_new: float32 [512, 128, 128], P(('section', 'row'))
- adjoint: float32 [512, 128, 128], P(('section', 'row'))
Inputs may be any that keep to these rules, and one draw needn't show every extreme that they name: `cross_owner`: among the 128 cross slots of one device, live or not, at most 16 name the same owner, a bound that some block reaches of them. `cross_count`: some device has all its cross slots live.
All inputs are finite; a program needn't handle non-finite values.
Results may differ from a plain program's by a relative error of at most 0.0089.
Values may be sent and summed in bfloat16 or wider, within the bound.
A program may use at most 192 MiB of HBM per device.

v0:
```python
import jax
import jax.numpy as jnp
from jax import lax
from jax.sharding import PartitionSpec as P

CAP = 16


precise = lax.Precision.HIGHEST


def shifted(x, axis, by):
    size = lax.axis_size(axis)
    pairs = [(i, i + by) for i in range(size) if 0 <= i + by < size]
    return lax.ppermute(x, axis, pairs)


def pivot_products(lower_factor_blocks, pivots, pivot_inverse):
    selected_entry = jnp.take(pivot_inverse, pivots, axis=0)
    return jnp.einsum(
        "zmq,zqy->zmy", lower_factor_blocks, selected_entry, preferred_element_type=jnp.float32
    ).astype(jnp.bfloat16)


def finish_products(rescaled_blocks, upper_factor_blocks):
    return jnp.einsum(
        "zmq,zqy->zmy", rescaled_blocks, upper_factor_blocks, preferred_element_type=jnp.float32
    ).astype(jnp.bfloat16)


def add_into_rows(blocks, targets, row_count):
    picks = (targets[None, :] == jnp.arange(row_count, dtype=jnp.float32)[:, None]).astype(
        jnp.bfloat16
    )
    return jnp.einsum("ks,sab->kab", picks, blocks, preferred_element_type=jnp.float32)


def apply_map(matrix, vector):
    return jnp.einsum("kab,knb->kna", matrix, vector, precision=precise)


def per_device(
    coupling,
    diag_inverse,
    pivot_inverse,
    cross_left,
    cross_right,
    cross_pivot,
    cross_owner,
    foreign_target_row,
    cross_count,
    local_left,
    local_right,
    local_pivot,
    local_target,
    adjoint_seed,
):
    row_count = coupling.shape[0]
    width = coupling.shape[1]
    groups = lax.axis_size("row")
    slots = cross_left.shape[0]
    capacity = CAP
    slot_index = jnp.arange(slots, dtype=jnp.int32)
    local_scaled = pivot_products(local_left, local_pivot, pivot_inverse)
    local_blocks = finish_products(local_scaled, local_right)
    local_sum = add_into_rows(local_blocks, local_target.astype(jnp.float32), row_count)
    owner = cross_owner[:, 0]
    earlier = (owner[None, :] == owner[:, None]) & (slot_index[None, :] < slot_index[:, None])
    position = owner * capacity + jnp.sum(earlier.astype(jnp.int32), axis=1)
    buffer_index = jnp.arange(groups * capacity, dtype=jnp.int32)
    matches = position[None, :] == buffer_index[:, None]
    filled = jnp.any(matches, axis=1)
    source = jnp.sum(jnp.where(matches, slot_index[None, :], 0), axis=1)
    live_target = jnp.where(slot_index < cross_count[0], foreign_target_row, -1)
    sent_target = (
        jnp.where(filled, jnp.take(live_target, source), -1)
        .astype(jnp.bfloat16)
        .reshape(groups, capacity)
    )
    cross_scaled = pivot_products(cross_left, cross_pivot, pivot_inverse)
    cross_blocks = finish_products(cross_scaled, cross_right)
    sent_blocks = jnp.take(cross_blocks, source, axis=0).reshape(groups, capacity, width, width)
    arrived, arrived_target = (
        lax.all_to_all(sent_blocks, "row", split_axis=0, concat_axis=0, tiled=True),
        lax.all_to_all(sent_target, "row", split_axis=0, concat_axis=0, tiled=True),
    )
    remote_sum = add_into_rows(
        arrived.reshape(groups * capacity, width, width),
        arrived_target.reshape(groups * capacity).astype(jnp.float32),
        row_count,
    )
    updated = coupling.astype(jnp.float32) - local_sum - remote_sum
    step_matrix = -jnp.einsum("kab,kbc->kac", diag_inverse, updated, precision=precise)
    step_offset = jnp.einsum("kab,knb->kna", diag_inverse, adjoint_seed, precision=precise)

    def advance(counter, current):
        after = shifted(current, "section", -1)
        return step_offset + apply_map(step_matrix, after)

    adjoint = lax.fori_loop(0, lax.axis_size("section") - 1, advance, step_offset)
    return (updated, adjoint)


def solution(mesh):
    return jax.shard_map(
        per_device,
        mesh=mesh,
        in_specs=(
            P(("section", "row"), None, None),
            P(("section", "row"), None, None),
            P(("section", "row"), None, None),
            P(("section", "row"), None, None),
            P(("section", "row"), None, None),
            P(("section", "row")),
            P(("section", "row"), None),
            P(("section", "row")),
            P(("section", "row")),
            P(("section", "row"), None, None),
            P(("section", "row"), None, None),
            P(("section", "row")),
            P(("section", "row")),
            P(("section", "row"), None, None),
        ),
        out_specs=(P(("section", "row"), None, None), P(("section", "row"), None, None)),
        check_vma=False,
    )
```

profile of v0, /device:TPU:1, one launch (start us, length us, event | category | flops | bytes accessed | tf_op | source)
XLA Modules:
  0.0 215.8 jit_solution(7484828459748510272)
XLA Ops:
  5.9 6.4 %all-to-all-start = ((bf16[8,1,16]{2,1,0:T(2,128)(2,1)}), bf16[8,1,16]{2,1,0:T(2,128)(2,1)S(1)}, u32[]{:S(2)}, u32[]{:S(2)}) async-start(bf16[8,1,16]{2,1,0:T(2,128)(2,1)} %copy.41), calls=%async_computation | async-start | bytes 8192 | tf_op jit(solution)/shard_map/all_to_all | solution.py:85
  13.7 4.0 %gather_fusion.3 = bf16[128,128,128]{2,1,0:T(8,128)(2,1)} fusion(bf16[4,128,128]{2,1,0:T(8,128)(2,1)} %param.20, s32[1024]{0:T(1024)S(1)} %pad_clamp_fusion), kind=kCustom, calls=%fused_computation.1.clone | custom fusion | bytes 8389120 | tf_op jit(solution)/shard_map/jit(_take)/gather | solution.py:19
  17.6 10.7 %fusion.25 = bf16[128,128,128]{2,1,0:T(8,128)(2,1)} fusion(bf16[128,128,128]{2,1,0:T(8,128)(2,1)} %param.22, bf16[128,128,128]{2,1,0:T(8,128)(2,1)} %param.21, bf16[128,128,128]{2,1,0:T(8,128)(2,1)} %gather_fusion.3, pred[128]{0:T(512)(128)(4,1)S(1)} %compare_and_fusion.1), kind=kOutput, calls=%fused_computation.19 | convolution fusion | flops 1080033280 | bytes 16777344 | tf_op jit(solution)/shard_map/zmq,zqy->zmy/dot_general | solution.py:26
  28.4 5.2 %gather_fusion.1 = bf16[128,128,128]{2,1,0:T(8,128)(2,1)} fusion(bf16[128,128,128]{2,1,0:T(8,128)(2,1)} %fusion.25, s32[1024]{0:T(1024)S(1)} %pad_clamp_fusion.1), kind=kCustom, calls=%fused_computation.3 | custom fusion | bytes 8389120 | tf_op jit(solution)/shard_map/jit(_take)/gather | solution.py:82
  33.6 4.6 %broadcast_select_fusion = bf16[8,16,128,128]{3,2,1,0:T(8,128)(2,1)} fusion(bf16[8,16,128,128]{3,2,1,0:T(8,128)(2,1)} %bitcast.33, pred[8,16]{1,0:T(8,128)(4,1)S(1)} %compare_and_fusion), kind=kLoop, calls=%fused_computation.17 | loop fusion | flops 2097152 | bytes 8388736 | tf_op jit(solution)/shard_map/jit(_take)/select_n | solution.py:82
  38.2 5.6 %all-to-all-start.1 = ((bf16[8,16,128,128]{3,2,1,0:T(8,128)(2,1)}), bf16[8,16,128,128]{3,2,1,0:T(8,128)(2,1)}, u32[]{:S(2)}, u32[]{:S(2)}) async-start(bf16[8,16,128,128]{3,2,1,0:T(8,128)(2,1)} %broadcast_select_fusion), calls=%async_computation.1 | async-start | bytes 8388608 | tf_op jit(solution)/shard_map/all_to_all | solution.py:84
  43.8 3.0 %gather_fusion.2 = bf16[128,128,128]{2,1,0:T(8,128)(2,1)} fusion(bf16[4,128,128]{2,1,0:T(8,128)(2,1)S(1)} %copy-done.1, s32[1024]{0:T(1024)S(1)} %pad_clamp_fusion.2), kind=kCustom, calls=%fused_computation.clone | custom fusion | bytes 8389120 | tf_op jit(solution)/shard_map/jit(_take)/gather | solution.py:19
  46.9 2.3 %fusion.55 = f32[16,128,128]{2,1,0:T(8,128)S(1)} fusion(f32[16,128,128]{2,1,0:T(8,128)S(1)} %copy-done.4, f32[16,128,128]{2,1,0:T(8,128)S(1)} %copy-done), kind=kOutput, calls=%fused_computation.57 | convolution fusion | flops 402653184 | bytes 3145728 | tf_op jit(solution)/shard_map/kab,knb->kna/dot_general | solution.py:94
  50.2 10.7 %fusion.20 = bf16[128,128,128]{2,1,0:T(8,128)(2,1)} fusion(bf16[128,128,128]{2,1,0:T(8,128)(2,1)} %param.28, bf16[128,128,128]{2,1,0:T(8,128)(2,1)} %param.27, bf16[128,128,128]{2,1,0:T(8,128)(2,1)} %gather_fusion.2, pred[128]{0:T(512)(128)(4,1)S(1)} %compare_and_fusion.2), kind=kOutput, calls=%fused_computation.18 | convolution fusion | flops 1080033280 | bytes 16777344 | tf_op jit(solution)/shard_map/zmq,zqy->zmy/dot_general | solution.py:26
  61.0 74.6 %all-to-all-done.1 = bf16[8,16,128,128]{3,2,1,0:T(8,128)(2,1)} async-done(((bf16[8,16,128,128]{3,2,1,0:T(8,128)(2,1)}), bf16[8,16,128,128]{3,2,1,0:T(8,128)(2,1)}, u32[]{:S(2)}, u32[]{:S(2)}) %all-to-all-start.1) | async-done | bytes 4194336 | tf_op jit(solution)/shard_map/all_to_all | solution.py:84
  135.6 4.9 %copy.44 = bf16[8,16,128,128]{3,1,0,2:T(8,128)(2,1)S(1)} copy(bf16[8,16,128,128]{3,2,1,0:T(8,128)(2,1)} %all-to-all-done.1) | data formatting | bytes 8388608 | tf_op jit(solution)/shard_map/all_to_all | solution.py:84
  142.8 2.7 %fusion.37 = f32[16,128,128]{2,0,1:T(8,128)S(1)} fusion(f32[16,128,128]{2,0,1:T(8,128)S(1)} %fusion.46, bf16[128,128,128]{2,1,0:T(8,128)(2,1)S(1)} %copy-done.2, bf16[16,128,128]{2,1,0:T(8,128)(2,1)S(1)} %copy-done.5, f32[128]{0:T(128)S(1)} %convert_element_type.47), kind=kOutput, calls=%fused_computation.23 | convolution fusion | flops 67897344 | bytes 6816256 | tf_op jit(solution)/shard_map/ks,sab->kab/dot_general | solution.py:35
  146.9 2.8 %fusion.40 = f32[16,128,128]{1,2,0:T(8,128)} fusion(f32[16,128,128]{2,1,0:T(8,128)S(1)} %copy.47, f32[16,128,128]{2,1,0:T(8,128)S(1)} %copy-done), kind=kOutput, calls=%fused_computation.25 | convolution fusion | flops 402915328 | bytes 3145728 | tf_op jit(solution)/shard_map/kab,kbc->kac/dot_general | solution.py:93
  149.7 1.6 copy.46
  151.2 64.5 %while.10 = (s32[]{:T(128)}, f32[16,128,128]{2,1,0:T(8,128)}, f32[16,128,128]{2,1,0:T(8,128)S(1)}, f32[16,128,128]{2,1,0:T(8,128)S(1)}, s32[]{:T(128)}) while((s32[]{:T(128)}, f32[16,128,128]{2,1,0:T(8,128)}, f32[16,128,128]{2,1,0:T(8,128)S(1)}, f32[16,128,128]{2,1,0:T(8,128)S(1)}, s32[]{:T(128)}) %tuple.31), condition=%wide.region_4.6_spmd, body=%wide.region_3.5_spmd.sunk | while | flops 402915328 | bytes 8388709 | solution.py:100
  151.3 4.3 %collective-permute-start = (f32[16,128,128]{2,1,0:T(8,128)}, f32[16,128,128]{2,1,0:T(8,128)}, u32[]{:S(2)}, u32[]{:S(2)}) collective-permute-start(f32[16,128,128]{2,1,0:T(8,128)} %get-tuple-element.89), channel_id=1, source_target_pairs={{8,0},{16,8},{24,16},{9,1},{17,9},{25,17},{10,2},{18,10},{26,18},{... | collective-permute-start | bytes 3145736 | tf_op jit(solution)/shard_map/while/body/eval_jaxpr/ppermute | solution.py:15
  155.6 13.9 %collective-permute-done = f32[16,128,128]{2,1,0:T(8,128)} collective-permute-done((f32[16,128,128]{2,1,0:T(8,128)}, f32[16,128,128]{2,1,0:T(8,128)}, u32[]{:S(2)}, u32[]{:S(2)}) %collective-permute-start) | collective-permute-done | bytes 1048608 | tf_op jit(solution)/shard_map/while/body/eval_jaxpr/ppermute | solution.py:15
  169.5 4.5 %convolution_add_fusion.2 = f32[16,128,128]{2,1,0:T(8,128)} fusion(f32[16,128,128]{2,1,0:T(8,128)S(1)} %get-tuple-element.96, f32[16,128,128]{2,1,0:T(8,128)} %collective-permute-done, f32[16,128,128]{2,1,0:T(8,128)S(1)} %get-tuple-element.95), kind=kOutput, calls=%fused_computation.4.clone.1 | convolution fusion | flops 402915328 | bytes 4194304 | tf_op jit(solution)/shard_map/while/body/eval_jaxpr/kab,knb->kna/dot_general | solution.py:39
  174.0 1.9 collective-permute-start
  175.9 14.5 %collective-permute-done = f32[16,128,128]{2,1,0:T(8,128)} collective-permute-done((f32[16,128,128]{2,1,0:T(8,128)}, f32[16,128,128]{2,1,0:T(8,128)}, u32[]{:S(2)}, u32[]{:S(2)}) %collective-permute-start) | collective-permute-done | bytes 1048608 | tf_op jit(solution)/shard_map/while/body/eval_jaxpr/ppermute | solution.py:15
  190.4 4.5 %convolution_add_fusion.2 = f32[16,128,128]{2,1,0:T(8,128)} fusion(f32[16,128,128]{2,1,0:T(8,128)S(1)} %get-tuple-element.96, f32[16,128,128]{2,1,0:T(8,128)} %collective-permute-done, f32[16,128,128]{2,1,0:T(8,128)S(1)} %get-tuple-element.95), kind=kOutput, calls=%fused_computation.4.clone.1 | convolution fusion | flops 402915328 | bytes 4194304 | tf_op jit(solution)/shard_map/while/body/eval_jaxpr/kab,knb->kna/dot_general | solution.py:39
  194.9 1.9 collective-permute-start
  196.8 14.5 %collective-permute-done = f32[16,128,128]{2,1,0:T(8,128)} collective-permute-done((f32[16,128,128]{2,1,0:T(8,128)}, f32[16,128,128]{2,1,0:T(8,128)}, u32[]{:S(2)}, u32[]{:S(2)}) %collective-permute-start) | collective-permute-done | bytes 1048608 | tf_op jit(solution)/shard_map/while/body/eval_jaxpr/ppermute | solution.py:15
  211.3 4.5 %convolution_add_fusion.2 = f32[16,128,128]{2,1,0:T(8,128)} fusion(f32[16,128,128]{2,1,0:T(8,128)S(1)} %get-tuple-element.96, f32[16,128,128]{2,1,0:T(8,128)} %collective-permute-done, f32[16,128,128]{2,1,0:T(8,128)S(1)} %get-tuple-element.95), kind=kOutput, calls=%fused_computation.4.clone.1 | convolution fusion | flops 402915328 | bytes 4194304 | tf_op jit(solution)/shard_map/while/body/eval_jaxpr/kab,knb->kna/dot_general | solution.py:39
  (44 shorter events, 10.7 us)
Async XLA Ops:
  0.6 46.2 %copy-start = (f32[16,128,128]{2,1,0:T(8,128)S(1)}, f32[16,128,128]{2,1,0:T(8,128)}, u32[]{:S(2)}) copy-start(f32[16,128,128]{2,1,0:T(8,128)} %param.19) | copy-start | bytes 3145732
  5.9 32.3 %all-to-all-start = ((bf16[8,1,16]{2,1,0:T(2,128)(2,1)}), bf16[8,1,16]{2,1,0:T(2,128)(2,1)S(1)}, u32[]{:S(2)}, u32[]{:S(2)}) async-start(bf16[8,1,16]{2,1,0:T(2,128)(2,1)} %copy.41), calls=%async_computation | async-start | bytes 8192 | tf_op jit(solution)/shard_map/all_to_all | solution.py:85
  38.2 5.6 %copy-start.7 = (s32[128]{0:T(128)S(1)}, s32[128]{0:T(128)}, u32[]{:S(2)}) copy-start(s32[128]{0:T(128)} %param.29) | copy-start | bytes 1540
  38.2 5.6 %copy-start.1 = (bf16[4,128,128]{2,1,0:T(8,128)(2,1)S(1)}, bf16[4,128,128]{2,1,0:T(8,128)(2,1)}, u32[]{:S(2)}) copy-start(bf16[4,128,128]{2,1,0:T(8,128)(2,1)} %param.20) | copy-start | bytes 393220
  38.2 97.4 %all-to-all-start.1 = ((bf16[8,16,128,128]{3,2,1,0:T(8,128)(2,1)}), bf16[8,16,128,128]{3,2,1,0:T(8,128)(2,1)}, u32[]{:S(2)}, u32[]{:S(2)}) async-start(bf16[8,16,128,128]{3,2,1,0:T(8,128)(2,1)} %broadcast_select_fusion), calls=%async_computation.1 | async-start | bytes 8388608 | tf_op jit(solution)/shard_map/all_to_all | solution.py:84
  43.8 3.1 %copy-start.6 = (s32[128]{0:T(128)S(1)}, s32[128]{0:T(128)}, u32[]{:S(2)}) copy-start(s32[128]{0:T(128)} %param.30) | copy-start | bytes 1540
  43.8 3.1 %copy-start.4 = (f32[16,128,128]{2,1,0:T(8,128)S(1)}, f32[16,128,128]{2,1,0:T(8,128)}, u32[]{:S(2)}) copy-start(f32[16,128,128]{2,1,0:T(8,128)} %param.31) | copy-start | bytes 3145732
  140.5 2.2 %copy-start.2 = (bf16[128,128,128]{2,1,0:T(8,128)(2,1)S(1)}, bf16[128,128,128]{2,1,0:T(8,128)(2,1)}, u32[]{:S(2)}) copy-start(bf16[128,128,128]{2,1,0:T(8,128)(2,1)} %fusion.20) | copy-start | bytes 12582916
  140.5 2.3 %copy-start.5 = (bf16[16,128,128]{2,1,0:T(8,128)(2,1)S(1)}, bf16[16,128,128]{2,1,0:T(8,128)(2,1)}, u32[]{:S(2)}) copy-start(bf16[16,128,128]{2,1,0:T(8,128)(2,1)} %param.18) | copy-start | bytes 1572868
  145.9 1.0 copy-start.3
  151.3 18.2 %collective-permute-start = (f32[16,128,128]{2,1,0:T(8,128)}, f32[16,128,128]{2,1,0:T(8,128)}, u32[]{:S(2)}, u32[]{:S(2)}) collective-permute-start(f32[16,128,128]{2,1,0:T(8,128)} %get-tuple-element.89), channel_id=1, source_target_pairs={{8,0},{16,8},{24,16},{9,1},{17,9},{25,17},{10,2},{18,10},{26,18},{... | collective-permute-start | bytes 3145736 | tf_op jit(solution)/shard_map/while/body/eval_jaxpr/ppermute | solution.py:15
  174.0 16.4 %collective-permute-start = (f32[16,128,128]{2,1,0:T(8,128)}, f32[16,128,128]{2,1,0:T(8,128)}, u32[]{:S(2)}, u32[]{:S(2)}) collective-permute-start(f32[16,128,128]{2,1,0:T(8,128)} %get-tuple-element.89), channel_id=1, source_target_pairs={{8,0},{16,8},{24,16},{9,1},{17,9},{25,17},{10,2},{18,10},{26,18},{... | collective-permute-start | bytes 3145736 | tf_op jit(solution)/shard_map/while/body/eval_jaxpr/ppermute | solution.py:15
  194.9 16.4 %collective-permute-start = (f32[16,128,128]{2,1,0:T(8,128)}, f32[16,128,128]{2,1,0:T(8,128)}, u32[]{:S(2)}, u32[]{:S(2)}) collective-permute-start(f32[16,128,128]{2,1,0:T(8,128)} %get-tuple-element.89), channel_id=1, source_target_pairs={{8,0},{16,8},{24,16},{9,1},{17,9},{25,17},{10,2},{18,10},{26,18},{... | collective-permute-start | bytes 3145736 | tf_op jit(solution)/shard_map/while/body/eval_jaxpr/ppermute | solution.py:15
where the time goes:
time: 216 us
  waiting for transfers between devices  118 us (55%)
  matrix products  43.4 us (20%)
  local copies, waits for them, and re-layouts  24.8 us (11%)
  starting transfers between devices  20.1 us (9%)
  other arithmetic  8.43 us (4%)
    all_to_all x1, waiting for transfers between devices, per_device(): lax.all_to_all(sent_blocks, 'row', split_axis=0, concat_axis=0, tiled=True)  74.6 us
    ppermute x3, waiting for transfers between devices, shifted(): return lax.ppermute(x, axis, pairs)  42.9 us
    dot_general x2, matrix products, finish_products(): jnp.einsum('zmq,zqy->zmy', rescaled_blocks, upper_factor_blocks, preferre...  21.5 us
    dot_general x3, matrix products, apply_map(): return jnp.einsum('kab,knb->kna', matrix, vector, precision=precise)  13.4 us
    ppermute x3, starting transfers between devices, shifted(): return lax.ppermute(x, axis, pairs)  8.13 us
    gather x2, local copies, waits for them, and re-layouts, pivot_products(): selected_entry = jnp.take(pivot_inverse, pivots, axis=0)  6.99 us
    all_to_all x1, starting transfers between devices, per_device(): lax.all_to_all(sent_target, 'row', split_axis=0, concat_axis=0, tiled=True)  6.35 us
    all_to_all x1, starting transfers between devices, per_device(): lax.all_to_all(sent_blocks, 'row', split_axis=0, concat_axis=0, tiled=True)  5.57 us
  transfers between devices with their start and end apart: 5, of which 4 were waited for; matrix products, arithmetic and copies ran while one was open for 20% of the time, Pallas kernels for 0%

commit v1 on v0

v1 whole, which is shorter than its diff:
```python
import functools

import jax
import jax.numpy as jnp
from jax import lax
from jax.experimental import pallas as pl
from jax.experimental.pallas import tpu as pltpu
from jax.sharding import PartitionSpec as P

STEP = 16
DEPTH = 4
HIGH = 4
LAG = 2
VMEM_LIMIT = 56 * 1024 * 1024
precise = lax.Precision.HIGHEST
MESH = pl.DeviceIdType.MESH


def products_kernel(
    low, rows, cpiv, cown, crow, ccount, lpiv, lrow,
    cl, cr, ll, lr, pinv, coup, part, base, acc,
):
    g = pl.program_id(0)
    targets = part.shape[0]

    @pl.when(g == 0)
    def _():
        def clear(i, carry):
            acc[i] = jnp.zeros(acc.shape[1:], acc.dtype)
            return carry

        lax.fori_loop(0, targets, clear, 0)
        base[...] = coup[...].astype(jnp.float32)

    live = ccount[0]
    for i in range(STEP):
        t = g * STEP + i
        owner = cown[t]
        spot = ((owner % low) * rows + crow[t]) * HIGH + owner // low
        spot = jnp.where(t < live, spot, targets)
        scaled = jnp.dot(cl[i], pinv[cpiv[t]], preferred_element_type=jnp.float32)
        update = jnp.dot(
            scaled.astype(jnp.bfloat16), cr[i], preferred_element_type=jnp.float32
        )
        acc[spot] += update
        scaled = jnp.dot(ll[i], pinv[lpiv[t]], preferred_element_type=jnp.float32)
        update = jnp.dot(
            scaled.astype(jnp.bfloat16), lr[i], preferred_element_type=jnp.float32
        )
        base[lrow[t]] -= update

    @pl.when(g == pl.num_programs(0) - 1)
    def _():
        def put(i, carry):
            part[i] = acc[i].astype(part.dtype)
            return carry

        lax.fori_loop(0, targets, put, 0)


def exchange_kernel(
    low, sections, part, base, diag, seed, new, adj,
    own, got_low, got_high, later, matrix,
    load_sem, ls, lr, hs, hr, vs, vr,
):
    rows = base.shape[0]
    row = lax.axis_index("row")
    sec = lax.axis_index("section")
    hi, lo = row // low, row % low

    load = pltpu.make_async_copy(part.at[lo], own, load_sem)
    load.start()

    barrier = pltpu.get_barrier_semaphore()
    for d in range(1, low):
        peer = hi * low + (lo + d) % low
        pl.semaphore_signal(barrier, inc=1, device_id={"row": peer}, device_id_type=MESH)
    for d in range(1, HIGH):
        peer = ((hi + d) % HIGH) * low + lo
        pl.semaphore_signal(barrier, inc=1, device_id={"row": peer}, device_id_type=MESH)

    @pl.when(sec > 0)
    def _():
        pl.semaphore_signal(
            barrier, inc=1, device_id={"section": sec - 1}, device_id_type=MESH
        )

    @pl.when(sec < sections - 1)
    def _():
        pl.semaphore_signal(
            barrier, inc=1, device_id={"section": sec + 1}, device_id_type=MESH
        )

    ends = jnp.where(sec > 0, 1, 0) + jnp.where(sec < sections - 1, 1, 0)
    pl.semaphore_wait(barrier, (low - 1) + (HIGH - 1) + ends)

    def low_copy(d, k):
        peer = (lo + d) % low
        return pltpu.make_async_remote_copy(
            src_ref=part.at[peer, k],
            dst_ref=got_low.at[d - 1, k],
            send_sem=ls.at[d - 1, k],
            recv_sem=lr.at[d - 1, k],
            device_id={"row": hi * low + peer},
            device_id_type=MESH,
        )

    def high_copy(d, k):
        peer = (hi + d) % HIGH
        return pltpu.make_async_remote_copy(
            src_ref=own.at[k, peer],
            dst_ref=got_high.at[d - 1, k],
            send_sem=hs.at[d - 1, k],
            recv_sem=hr.at[d - 1, k],
            device_id={"row": peer * low + lo},
            device_id_type=MESH,
        )

    def chain_copy(k, target):
        return pltpu.make_async_remote_copy(
            src_ref=adj.at[k],
            dst_ref=later.at[k],
            send_sem=vs.at[k],
            recv_sem=vr.at[k],
            device_id={"section": target},
            device_id_type=MESH,
        )

    for k in range(DEPTH):
        for d in range(1, low):
            low_copy(d, k).start()

    def offset(k, carry):
        adj[k] = lax.dot_general(
            seed[k], diag[k], (((1,), (1,)), ((), ())),
            precision=precise, preferred_element_type=jnp.float32,
        )

        @pl.when(sec == sections - 1)
        def _():
            chain_copy(k, sec - 1).start()

        return carry

    lax.fori_loop(0, rows, offset, 0)
    load.wait()

    def step(c, carry):
        @pl.when(c + DEPTH < rows)
        def _():
            for d in range(1, low):
                low_copy(d, c + DEPTH).start()

        @pl.when(c < rows)
        def _():
            for d in range(1, low):
                low_copy(d, c).wait_recv()
            for h in range(HIGH):
                total = own[c, h].astype(jnp.float32)
                for d in range(1, low):
                    total += got_low[d - 1, c, h].astype(jnp.float32)
                own[c, h] = total.astype(own.dtype)
            for d in range(1, HIGH):
                high_copy(d, c).start()

        j = c - LAG

        @pl.when((j >= 0) & (j < rows))
        def _():
            for d in range(1, HIGH):
                high_copy(d, j).wait_recv()
            total = own[j, hi].astype(jnp.float32)
            for d in range(1, HIGH):
                total += got_high[d - 1, j].astype(jnp.float32)
            total = base[j] - total
            new[j] = total
            matrix[j] = jnp.dot(
                diag[j], total, precision=precise, preferred_element_type=jnp.float32
            )

        m = c - LAG - (sections - 2 - sec)

        @pl.when((sec < sections - 1) & (m >= 0) & (m < rows))
        def _():
            chain_copy(m, sec).wait_recv()
            adj[m] -= lax.dot_general(
                later[m], matrix[m], (((1,), (1,)), ((), ())),
                precision=precise, preferred_element_type=jnp.float32,
            )

            @pl.when(sec > 0)
            def _():
                chain_copy(m, sec - 1).start()

        return carry

    lax.fori_loop(0, rows + LAG + sections - 2, step, 0)

    def drain(k, carry):
        for d in range(1, low):
            low_copy(d, k).wait_send()
        for d in range(1, HIGH):
            high_copy(d, k).wait_send()

        @pl.when(sec > 0)
        def _():
            chain_copy(k, sec - 1).wait_send()

        return carry

    lax.fori_loop(0, rows, drain, 0)


def per_device(
    coupling,
    diag_inverse,
    pivot_inverse,
    cross_left,
    cross_right,
    cross_pivot,
    cross_owner,
    foreign_target_row,
    cross_count,
    local_left,
    local_right,
    local_pivot,
    local_target,
    adjoint_seed,
):
    rows, width, _ = coupling.shape
    groups = lax.axis_size("row")
    sections = lax.axis_size("section")
    low = groups // HIGH
    slots = cross_left.shape[0]
    targets = groups * rows
    block = (width, width)

    def whole(shape):
        return pl.BlockSpec(shape, lambda g, *_: (0,) * len(shape))

    def streamed():
        return pl.BlockSpec((STEP,) + block, lambda g, *_: (g, 0, 0))

    part, base = pl.pallas_call(
        functools.partial(products_kernel, low, rows),
        out_shape=(
            jax.ShapeDtypeStruct((targets,) + block, jnp.bfloat16),
            jax.ShapeDtypeStruct((rows,) + block, jnp.float32),
        ),
        grid_spec=pltpu.PrefetchScalarGridSpec(
            num_scalar_prefetch=6,
            grid=(slots // STEP,),
            in_specs=[streamed(), streamed(), streamed(), streamed(),
                      whole(pivot_inverse.shape), whole(coupling.shape)],
            out_specs=[whole((targets,) + block), whole((rows,) + block)],
            scratch_shapes=[pltpu.VMEM((targets + 1,) + block, jnp.float32)],
        ),
        compiler_params=pltpu.CompilerParams(
            dimension_semantics=("arbitrary",), vmem_limit_bytes=VMEM_LIMIT
        ),
        cost_estimate=pl.CostEstimate(
            flops=8 * slots * width ** 3, bytes_accessed=22 * 1024 * 1024, transcendentals=0
        ),
        name="products",
    )(cross_pivot, cross_owner[:, 0], foreign_target_row, cross_count, local_pivot,
      local_target, cross_left, cross_right, local_left, local_right, pivot_inverse, coupling)

    part = part.reshape((low, rows, HIGH) + block)
    vmem = pl.BlockSpec(memory_space=pltpu.VMEM)
    dma = pltpu.SemaphoreType.DMA
    return pl.pallas_call(
        functools.partial(exchange_kernel, low, sections),
        out_shape=(
            jax.ShapeDtypeStruct((rows,) + block, jnp.float32),
            jax.ShapeDtypeStruct((rows,) + block, jnp.float32),
        ),
        in_specs=[pl.BlockSpec(memory_space=pl.ANY), vmem, vmem, vmem],
        out_specs=(vmem, vmem),
        scratch_shapes=[
            pltpu.VMEM((rows, HIGH) + block, jnp.bfloat16),
            pltpu.VMEM((low - 1, rows, HIGH) + block, jnp.bfloat16),
            pltpu.VMEM((HIGH - 1, rows) + block, jnp.bfloat16),
            pltpu.VMEM((rows,) + block, jnp.float32),
            pltpu.VMEM((rows,) + block, jnp.float32),
            dma(()),
            dma((low - 1, rows)),
            dma((low - 1, rows)),
            dma((HIGH - 1, rows)),
            dma((HIGH - 1, rows)),
            dma((rows,)),
            dma((rows,)),
        ],
        compiler_params=pltpu.CompilerParams(
            collective_id=0, has_side_effects=True, vmem_limit_bytes=VMEM_LIMIT
        ),
        name="exchange",
    )(part, base, diag_inverse, adjoint_seed)


def solution(mesh):
    spread = P(("section", "row"))
    return jax.shard_map(
        per_device,
        mesh=mesh,
        in_specs=(spread,) * 14,
        out_specs=(spread, spread),
        check_vma=False,
    )
```

time: 216 us -> 88.4 us (0.41)
  waiting for transfers between devices: 118 us -> 0 us
  Pallas kernels: 0 us -> 81.4 us
  matrix products: 43.4 us -> 0 us
  local copies, waits for them, and re-layouts: 24.8 us -> 4.59 us
  starting transfers between devices: 20.1 us -> 0 us
  other arithmetic: 8.43 us -> 0 us
    pallas_call x0 -> x2, Pallas kernels: none -> 81.4 us  [the longest x1 65.7 us: per_device(): pl.pallas_call(functools.partial(exchange_kernel, low, sections), out_sha...]
    all_to_all x2 -> x0, waiting for transfers between devices: 74.6 us -> none  [the longest x1 74.6 us: per_device(): lax.all_to_all(sent_blocks, 'row', split_axis=0, concat_axis=0, tiled=True)]
    dot_general x9 -> x0, matrix products: 43.4 us -> none  [the longest x2 21.5 us: finish_products(): jnp.einsum('zmq,zqy->zmy', rescaled_blocks, upper_factor_blocks, preferre...]
    ppermute x3 -> x0, waiting for transfers between devices: 42.9 us -> none  [shifted(): return lax.ppermute(x, axis, pairs)]
    gather x5 -> x0, local copies, waits for them, and re-layouts: 13.5 us -> none  [the longest x2 6.99 us: pivot_products(): selected_entry = jnp.take(pivot_inverse, pivots, axis=0)]
    all_to_all x2 -> x0, starting transfers between devices: 11.9 us -> none  [the longest x1 6.35 us: per_device(): lax.all_to_all(sent_target, 'row', split_axis=0, concat_axis=0, tiled=True)]
    ppermute x3 -> x0, starting transfers between devices: 8.13 us -> none  [shifted(): return lax.ppermute(x, axis, pairs)]
    select_n x5 -> x0, other arithmetic: 5.89 us -> none  [the longest x1 4.57 us: per_device(): jnp.take(cross_blocks, source, axis=0)]
  transfers between devices with their start and end apart: 5 -> 0, of which waited for: 4 -> 0; matrix products, arithmetic and copies ran while one was open for 20% -> 0% of each run, Pallas kernels for 0% -> 0%
where the time goes in v1:
time: 88.4 us; the launch traced here: 87.3 us
  Pallas kernels  81.4 us (92%)
  local copies, waits for them, and re-layouts  4.59 us (5%)
  between operations  1.29 us (1%)
    pallas_call x1, Pallas kernels, per_device(): pl.pallas_call(functools.partial(exchange_kernel, low, sections), out_sha...  65.7 us
    pallas_call x1, Pallas kernels, per_device(): pl.pallas_call(functools.partial(products_kernel, low, rows), out_shape=(...  15.7 us
    unnamed x2, local copies, waits for them, and re-layouts  4.59 us

profile of v1, /device:TPU:1, one launch (start us, length us, event | category | flops | bytes accessed | tf_op | source)
XLA Modules:
  0.0 87.3 jit_solution(7806418432494136060)
XLA Ops:
  1.3 15.7 %products.1 = (bf16[128,128,128]{2,1,0:T(8,128)(2,1)}, f32[16,128,128]{2,1,0:T(8,128)}) custom-call(s32[128]{0:T(128)} %cpiv.1, s32[128]{0:T(128)} %bitcast.3, s32[128]{0:T(128)} %crow.1, s32[1]{0:T(128)S(6)} %copy.18.ccount, s32[128]{0:T(128)} %lpiv.1, s32[128]{0:T(128)} %lrow.1, bf16[128,128,128]{2,1,0:T(8,128)(2,1)} %cl.1, bf16[128,128,128]{2,1,0:T(8,128)(2,1)} %cr.1, ...), custom_call_target="tpu_custom_call" | custom-call | flops 2147483648 | bytes 23068672 | tf_op jit(solution)/shard_map/products/pallas_call | solution.py:244
  17.0 65.7 %exchange.1 = (f32[16,128,128]{2,1,0:T(8,128)}, f32[16,128,128]{2,1,0:T(8,128)}) custom-call(bf16[2,16,4,128,128]{4,3,2,1,0:T(8,128)(2,1)} %bitcast.2, f32[16,128,128]{2,1,0:T(8,128)} %get-tuple-element.5.base, f32[16,128,128]{2,1,0:T(8,128)} %diag.1, f32[16,128,128]{2,1,0:T(8,128)} %seed.1), custom_call_target="tpu_custom_call" | custom-call | tf_op jit(solution)/shard_map/exchange/pallas_call | solution.py:271
  82.7 2.3 %copy.19 = f32[16,128,128]{2,1,0:T(8,128)} copy(f32[16,128,128]{2,1,0:T(8,128)} %get-tuple-element.8) | data formatting | bytes 2097152
  85.0 2.3 %copy.20 = f32[16,128,128]{2,1,0:T(8,128)} copy(f32[16,128,128]{2,1,0:T(8,128)} %get-tuple-element.9) | data formatting | bytes 2097152

commit v2 on v1

--- a/solution.py
+++ b/solution.py
@@ -8,6 +8,8 @@
 from jax.sharding import PartitionSpec as P
 
 STEP = 16
+GROUP = 4
+LOCAL_GROUP = 4
 DEPTH = 4
 HIGH = 4
 LAG = 2
@@ -18,7 +20,7 @@
 
 def products_kernel(
     low, rows, cpiv, cown, crow, ccount, lpiv, lrow,
-    cl, cr, ll, lr, pinv, coup, part, base, acc,
+    cl, cr, pinv, part, index, acc,
 ):
     g = pl.program_id(0)
     targets = part.shape[0]
@@ -30,24 +32,26 @@
             return carry
 
         lax.fori_loop(0, targets, clear, 0)
-        base[...] = coup[...].astype(jnp.float32)
+        index[...] = local_order(lpiv[...], lrow[...])
 
     live = ccount[0]
-    for i in range(STEP):
-        t = g * STEP + i
-        owner = cown[t]
-        spot = ((owner % low) * rows + crow[t]) * HIGH + owner // low
-        spot = jnp.where(t < live, spot, targets)
-        scaled = jnp.dot(cl[i], pinv[cpiv[t]], preferred_element_type=jnp.float32)
-        update = jnp.dot(
-            scaled.astype(jnp.bfloat16), cr[i], preferred_element_type=jnp.float32
-        )
-        acc[spot] += update
-        scaled = jnp.dot(ll[i], pinv[lpiv[t]], preferred_element_type=jnp.float32)
-        update = jnp.dot(
-            scaled.astype(jnp.bfloat16), lr[i], preferred_element_type=jnp.float32
-        )
-        base[lrow[t]] -= update
+    for first in range(0, STEP, GROUP):
+        picked = range(first, first + GROUP)
+        scaled = [
+            jnp.dot(
+                cl[i], pinv[cpiv[g * STEP + i]], preferred_element_type=jnp.float32
+            ).astype(jnp.bfloat16)
+            for i in picked
+        ]
+        updates = [
+            jnp.dot(half, cr[i], preferred_element_type=jnp.float32)
+            for half, i in zip(scaled, picked)
+        ]
+        for update, i in zip(updates, picked):
+            t = g * STEP + i
+            owner = cown[t]
+            spot = ((owner % low) * rows + crow[t]) * HIGH + owner // low
+            acc[jnp.where(t < live, spot, targets)] += update
 
     @pl.when(g == pl.num_programs(0) - 1)
     def _():
@@ -58,18 +62,69 @@
         lax.fori_loop(0, targets, put, 0)
 
 
+def local_order(pivot, row):
+    n = row.shape[1]
+    lane = lax.broadcasted_iota(jnp.int32, (n, n), 1).astype(jnp.float32)
+    slot = lax.broadcasted_iota(jnp.int32, (n, n), 0).astype(jnp.float32)
+
+    def down(x):
+        return jnp.broadcast_to(x, (n, n)).T
+
+    def total(x):
+        return jnp.sum(x, axis=0, keepdims=True)
+
+    row = row.astype(jnp.float32)
+    key = row * n + lane[:1]
+    rank = total(jnp.where(down(key) < key, 1.0, 0.0))
+    hit = down(rank) == lane
+    rows_down = down(row)
+    order = total(jnp.where(hit, slot, 0.0))
+    pivots = total(jnp.where(hit, down(pivot.astype(jnp.float32)), 0.0))
+    sorted_rows = total(jnp.where(hit, rows_down, 0.0))
+    last = total(jnp.where(rows_down <= lane, 1.0, 0.0)) - 1.0
+    count = total(jnp.where(rows_down == lane, 1.0, 0.0))
+    blank = jnp.zeros((3, n), jnp.float32)
+    return jnp.concatenate(
+        [order, pivots, sorted_rows, last, count, blank], axis=0
+    ).astype(jnp.int32)
+
+
+def results_kernel(new_in, adj_in, new_out, adj_out, sems):
+    pieces = sems.shape[1]
+    size = new_in.shape[0] // pieces
+    copies = []
+    for a, (source, target) in enumerate(((new_in, new_out), (adj_in, adj_out))):
+        for p in range(pieces):
+            span = pl.ds(p * size, size)
+            copies.append(
+                pltpu.make_async_copy(source.at[span], target.at[span], sems.at[a, p])
+            )
+    for copy in copies:
+        copy.start()
+    for copy in copies:
+        copy.wait()
+
+
 def exchange_kernel(
-    low, sections, part, base, diag, seed, new, adj,
+    low, sections, index, part, coup_hbm, diag_hbm, seed_hbm, pinv_hbm, left_hbm, right_hbm,
+    new, adj,
     own, got_low, got_high, later, matrix,
+    base, coup, diag, seed, pinv, left, right, sums,
     load_sem, ls, lr, hs, hr, vs, vr,
 ):
-    rows = base.shape[0]
+    rows, width, _ = base.shape
+    slots = left.shape[0]
     row = lax.axis_index("row")
     sec = lax.axis_index("section")
     hi, lo = row // low, row % low
 
-    load = pltpu.make_async_copy(part.at[lo], own, load_sem)
-    load.start()
+    loads = [
+        pltpu.make_async_copy(source, target, load_sem.at[i])
+        for i, (source, target) in enumerate((
+            (seed_hbm, seed), (diag_hbm, diag), (pinv_hbm, pinv), (left_hbm, left),
+            (right_hbm, right), (coup_hbm, coup), (part.at[lo], own),
+        ))
+    ]
 
     barrier = pltpu.get_barrier_semaphore()
     for d in range(1, low):
@@ -130,6 +185,11 @@
         for d in range(1, low):
             low_copy(d, k).start()
 
+    for load in loads:
+        load.start()
+    loads[0].wait()
+    loads[1].wait()
+
     def offset(k, carry):
         adj[k] = lax.dot_general(
             seed[k], diag[k], (((1,), (1,)), ((), ())),
@@ -143,7 +203,38 @@
         return carry
 
     lax.fori_loop(0, rows, offset, 0)
-    load.wait()
+    for load in loads[2:]:
+        load.wait()
+
+    def local_group(g, run):
+        at = [g * LOCAL_GROUP + i for i in range(LOCAL_GROUP)]
+        scaled = [
+            jnp.dot(
+                left[index[0, j]], pinv[index[1, j]], preferred_element_type=jnp.float32
+            ).astype(jnp.bfloat16)
+            for j in at
+        ]
+        updates = [
+            jnp.dot(half, right[index[0, j]], preferred_element_type=jnp.float32)
+            for half, j in zip(scaled, at)
+        ]
+        for update, j in zip(updates, at):
+            same = index[2, j] == index[2, jnp.maximum(j - 1, 0)]
+            run = run * jnp.where(same, 1.0, 0.0) + update
+            sums[j] = run
+        return run
+
+    lax.fori_loop(
+        0, slots // LOCAL_GROUP, local_group, jnp.zeros((width, width), jnp.float32)
+    )
+
+    def local_row(k, carry):
+        used = jnp.where(index[4, k] > 0, 1.0, 0.0)
+        total = sums[jnp.maximum(index[3, k], 0)] * used
+        base[k] = coup[k].astype(jnp.float32) - total
+        return carry
+
+    lax.fori_loop(0, rows, local_row, 0)
 
     def step(c, carry):
         @pl.when(c + DEPTH < rows)
@@ -231,7 +322,7 @@
     groups = lax.axis_size("row")
     sections = lax.axis_size("section")
     low = groups // HIGH
-    slots = cross_left.shape[0]
+    slots, local_slots = cross_left.shape[0], local_left.shape[0]
     targets = groups * rows
     block = (width, width)
 
@@ -241,40 +332,43 @@
     def streamed():
         return pl.BlockSpec((STEP,) + block, lambda g, *_: (g, 0, 0))
 
-    part, base = pl.pallas_call(
+    part, index = pl.pallas_call(
         functools.partial(products_kernel, low, rows),
         out_shape=(
             jax.ShapeDtypeStruct((targets,) + block, jnp.bfloat16),
-            jax.ShapeDtypeStruct((rows,) + block, jnp.float32),
+            jax.ShapeDtypeStruct((8, local_slots), jnp.int32),
         ),
         grid_spec=pltpu.PrefetchScalarGridSpec(
-            num_scalar_prefetch=6,
+            num_scalar_prefetch=4,
             grid=(slots // STEP,),
-            in_specs=[streamed(), streamed(), streamed(), streamed(),
-                      whole(pivot_inverse.shape), whole(coupling.shape)],
-            out_specs=[whole((targets,) + block), whole((rows,) + block)],
+            in_specs=[whole((1, local_slots)), whole((1, local_slots)),
+                      streamed(), streamed(), whole(pivot_inverse.shape)],
+            out_specs=[whole((targets,) + block), whole((8, local_slots))],
             scratch_shapes=[pltpu.VMEM((targets + 1,) + block, jnp.float32)],
         ),
         compiler_params=pltpu.CompilerParams(
             dimension_semantics=("arbitrary",), vmem_limit_bytes=VMEM_LIMIT
         ),
         cost_estimate=pl.CostEstimate(
-            flops=8 * slots * width ** 3, bytes_accessed=22 * 1024 * 1024, transcendentals=0
+            flops=4 * slots * width ** 3, bytes_accessed=12 * 1024 * 1024, transcendentals=0
         ),
         name="products",
-    )(cross_pivot, cross_owner[:, 0], foreign_target_row, cross_count, local_pivot,
-      local_target, cross_left, cross_right, local_left, local_right, pivot_inverse, coupling)
+    )(cross_pivot, cross_owner[:, 0], foreign_target_row, cross_count,
+      local_pivot.reshape(1, local_slots), local_target.reshape(1, local_slots),
+      cross_left, cross_right, pivot_inverse)
 
     part = part.reshape((low, rows, HIGH) + block)
     vmem = pl.BlockSpec(memory_space=pltpu.VMEM)
+    hbm = pl.BlockSpec(memory_space=pl.ANY)
     dma = pltpu.SemaphoreType.DMA
-    return pl.pallas_call(
+    outs = (
+        jax.ShapeDtypeStruct((rows,) + block, jnp.float32),
+        jax.ShapeDtypeStruct((rows,) + block, jnp.float32),
+    )
+    results = pl.pallas_call(
         functools.partial(exchange_kernel, low, sections),
-        out_shape=(
-            jax.ShapeDtypeStruct((rows,) + block, jnp.float32),
-            jax.ShapeDtypeStruct((rows,) + block, jnp.float32),
-        ),
-        in_specs=[pl.BlockSpec(memory_space=pl.ANY), vmem, vmem, vmem],
+        out_shape=outs,
+        in_specs=[pl.BlockSpec(memory_space=pltpu.SMEM)] + [hbm] * 7,
         out_specs=(vmem, vmem),
         scratch_shapes=[
             pltpu.VMEM((rows, HIGH) + block, jnp.bfloat16),
@@ -282,7 +376,15 @@
             pltpu.VMEM((HIGH - 1, rows) + block, jnp.bfloat16),
             pltpu.VMEM((rows,) + block, jnp.float32),
             pltpu.VMEM((rows,) + block, jnp.float32),
-            dma(()),
+            pltpu.VMEM((rows,) + block, jnp.float32),
+            pltpu.VMEM(coupling.shape, coupling.dtype),
+            pltpu.VMEM(diag_inverse.shape, jnp.float32),
+            pltpu.VMEM(adjoint_seed.shape, jnp.float32),
+            pltpu.VMEM(pivot_inverse.shape, pivot_inverse.dtype),
+            pltpu.VMEM(local_left.shape, local_left.dtype),
+            pltpu.VMEM(local_right.shape, local_right.dtype),
+            pltpu.VMEM((local_slots,) + block, jnp.float32),
+            dma((7,)),
             dma((low - 1, rows)),
             dma((low - 1, rows)),
             dma((HIGH - 1, rows)),
@@ -294,7 +396,16 @@
             collective_id=0, has_side_effects=True, vmem_limit_bytes=VMEM_LIMIT
         ),
         name="exchange",
-    )(part, base, diag_inverse, adjoint_seed)
+    )(index, part, coupling, diag_inverse, adjoint_seed, pivot_inverse, local_left, local_right)
+    return pl.pallas_call(
+        results_kernel,
+        out_shape=outs,
+        in_specs=[hbm, hbm],
+        out_specs=(hbm, hbm),
+        scratch_shapes=[dma((2, 4))],
+        compiler_params=pltpu.CompilerParams(vmem_limit_bytes=VMEM_LIMIT),
+        name="results",
+    )(*results)
 
 
 def solution(mesh):

time: 88.4 us -> 157 us (1.78)
  Pallas kernels: 81.4 us -> 155 us
  local copies, waits for them, and re-layouts: 4.59 us -> 0 us
    pallas_call x0 -> x1, Pallas kernels: none -> 64.7 us  [per_device(): pl.pallas_call(results_kernel, out_shape=outs, in_specs=[hbm, hbm], out_s...]
    pallas_call x1, Pallas kernels: 65.7 us -> 76.1 us  [per_device(): pl.pallas_call(functools.partial(exchange_kernel, low, sections), out_sha...]
    unnamed x2 -> x0, local copies, waits for them, and re-layouts: 4.59 us -> none
    pallas_call x1, Pallas kernels: 15.7 us -> 13.8 us  [per_device(): pl.pallas_call(functools.partial(products_kernel, low, rows), out_shape=(...]
where the time goes in v2:
time: 157 us; the launch traced here: 156 us
  Pallas kernels  155 us (99%)
    pallas_call x1, Pallas kernels, per_device(): pl.pallas_call(functools.partial(exchange_kernel, low, sections), out_sha...  76.1 us
    pallas_call x1, Pallas kernels, per_device(): pl.pallas_call(results_kernel, out_shape=outs, in_specs=[hbm, hbm], out_s...  64.7 us
    pallas_call x1, Pallas kernels, per_device(): pl.pallas_call(functools.partial(products_kernel, low, rows), out_shape=(...  13.8 us

profile of v2, /device:TPU:1, one launch (start us, length us, event | category | flops | bytes accessed | tf_op | source)
XLA Modules:
  0.0 155.9 jit_solution(1577591263786325041)
XLA Ops:
  1.3 13.8 %products.1 = (bf16[128,128,128]{2,1,0:T(8,128)(2,1)}, s32[8,128]{1,0:T(8,128)}) custom-call(s32[128]{0:T(128)} %cpiv.1, s32[128]{0:T(128)} %bitcast.5, s32[128]{0:T(128)} %crow.1, s32[1]{0:T(128)S(6)} %copy.16.ccount, s32[1,128]{1,0:T(1,128)} %bitcast.6, s32[1,128]{1,0:T(1,128)} %bitcast.7, bf16[128,128,128]{2,1,0:T(8,128)(2,1)} %cl.1, ...), custom_call_target="tpu_custom_call" | custom-call | flops 1073741824 | bytes 12582912 | tf_op jit(solution)/shard_map/products/pallas_call | solution.py:335
  15.0 76.1 %exchange.1 = (f32[16,128,128]{2,1,0:T(8,128)}, f32[16,128,128]{2,1,0:T(8,128)}) custom-call(s32[8,128]{1,0:T(8,128)} %get-tuple-element.6.index, bf16[2,16,4,128,128]{4,3,2,1,0:T(8,128)(2,1)} %bitcast.4, bf16[16,128,128]{2,1,0:T(8,128)(2,1)} %coup_hbm.1, f32[16,128,128]{2,1,0:T(8,128)} %diag_hbm.1, f32[16,128,128]{2,1,0:T(8,128)} %seed_hbm.1, ...), custom_call_target="tpu_custom_call" | custom-call | tf_op jit(solution)/shard_map/exchange/pallas_call | solution.py:368
  91.2 64.7 %results.1 = (f32[16,128,128]{2,1,0:T(8,128)}, f32[16,128,128]{2,1,0:T(8,128)}) custom-call(f32[16,128,128]{2,1,0:T(8,128)} %get-tuple-element.8.new_in, f32[16,128,128]{2,1,0:T(8,128)} %get-tuple-element.9.adj_in), custom_call_target="tpu_custom_call" | custom-call | tf_op jit(solution)/shard_map/results/pallas_call | solution.py:400

commit v3 on v2

--- a/solution.py
+++ b/solution.py
@@ -7,20 +7,21 @@
 from jax.experimental.pallas import tpu as pltpu
 from jax.sharding import PartitionSpec as P
 
-STEP = 16
+STEP = 32
 GROUP = 4
 LOCAL_GROUP = 4
 DEPTH = 4
 HIGH = 4
 LAG = 2
+LOCAL_STEPS = 4
+WRITES = 8
 VMEM_LIMIT = 56 * 1024 * 1024
-precise = lax.Precision.HIGHEST
 MESH = pl.DeviceIdType.MESH
 
 
 def products_kernel(
     low, rows, cpiv, cown, crow, ccount, lpiv, lrow,
-    cl, cr, pinv, part, index, acc,
+    cl, cr, pinv, part, index, acc, rounded, sems,
 ):
     g = pl.program_id(0)
     targets = part.shape[0]
@@ -31,7 +32,7 @@
             acc[i] = jnp.zeros(acc.shape[1:], acc.dtype)
             return carry
 
-        lax.fori_loop(0, targets, clear, 0)
+        lax.fori_loop(0, targets, clear, 0, unroll=8)
         index[...] = local_order(lpiv[...], lrow[...])
 
     live = ccount[0]
@@ -55,11 +56,22 @@
 
     @pl.when(g == pl.num_programs(0) - 1)
     def _():
-        def put(i, carry):
-            part[i] = acc[i].astype(part.dtype)
-            return carry
-
-        lax.fori_loop(0, targets, put, 0)
+        size = targets // WRITES
+
+        def write(n):
+            span = pl.ds(n * size, size)
+            return pltpu.make_async_copy(rounded.at[span], part.at[span], sems.at[n])
+
+        for n in range(WRITES):
+
+            def put(i, carry):
+                rounded[n * size + i] = acc[n * size + i].astype(rounded.dtype)
+                return carry
+
+            lax.fori_loop(0, size, put, 0, unroll=8)
+            write(n).start()
+        for n in range(WRITES):
+            write(n).wait()
 
 
 def local_order(pivot, row):
@@ -89,28 +101,46 @@
     ).astype(jnp.int32)
 
 
-def results_kernel(new_in, adj_in, new_out, adj_out, sems):
-    pieces = sems.shape[1]
+def results_kernel(new_in, adj_in, new_out, adj_out, held, in_sems, out_sems):
+    pieces = in_sems.shape[1]
     size = new_in.shape[0] // pieces
-    copies = []
+    reads, writes = [], []
     for a, (source, target) in enumerate(((new_in, new_out), (adj_in, adj_out))):
         for p in range(pieces):
             span = pl.ds(p * size, size)
-            copies.append(
-                pltpu.make_async_copy(source.at[span], target.at[span], sems.at[a, p])
+            reads.append(
+                pltpu.make_async_copy(source.at[span], held.at[a, span], in_sems.at[a, p])
             )
-    for copy in copies:
-        copy.start()
-    for copy in copies:
-        copy.wait()
+            writes.append(
+                pltpu.make_async_copy(held.at[a, span], target.at[span], out_sems.at[a, p])
+            )
+    for read in reads:
+        read.start()
+    for read, write in zip(reads, writes):
+        read.wait()
+        write.start()
+    for write in writes:
+        write.wait()
+
+
+def split(x):
+    high = x.astype(jnp.bfloat16)
+    return high, (x - high.astype(jnp.float32)).astype(jnp.bfloat16)
+
+
+def three_products(left, right, contract):
+    def one(a, b):
+        return lax.dot_general(a, b, (contract, ((), ())), preferred_element_type=jnp.float32)
+
+    return one(left[0], right[0]) + (one(left[0], right[1]) + one(left[1], right[0]))
 
 
 def exchange_kernel(
     low, sections, index, part, coup_hbm, diag_hbm, seed_hbm, pinv_hbm, left_hbm, right_hbm,
-    new, adj,
-    own, got_low, got_high, later, matrix,
-    base, coup, diag, seed, pinv, left, right, sums,
-    load_sem, ls, lr, hs, hr, vs, vr,
+    new_hbm, adj_hbm,
+    own, got_low, got_high, later, matrix_high, matrix_low, new, adj,
+    base, coup, diag, seed, pinv, left, right, sums, running,
+    load_sem, ls, lr, hs, hr, vs, vr, ns, ads,
 ):
     rows, width, _ = base.shape
     slots = left.shape[0]
@@ -121,8 +151,8 @@
     loads = [
         pltpu.make_async_copy(source, target, load_sem.at[i])
         for i, (source, target) in enumerate((
-            (seed_hbm, seed), (diag_hbm, diag), (pinv_hbm, pinv), (left_hbm, left),
-            (right_hbm, right), (coup_hbm, coup), (part.at[lo], own),
+            (part.at[lo], own), (seed_hbm, seed), (diag_hbm, diag), (pinv_hbm, pinv),
+            (left_hbm, left), (right_hbm, right), (coup_hbm, coup),
         ))
     ]
 
@@ -187,24 +217,14 @@
 
     for load in loads:
         load.start()
+    running[...] = jnp.zeros_like(running)
     loads[0].wait()
-    loads[1].wait()
-
-    def offset(k, carry):
-        adj[k] = lax.dot_general(
-            seed[k], diag[k], (((1,), (1,)), ((), ())),
-            precision=precise, preferred_element_type=jnp.float32,
-        )
-
-        @pl.when(sec == sections - 1)
-        def _():
-            chain_copy(k, sec - 1).start()
-
-        return carry
-
-    lax.fori_loop(0, rows, offset, 0)
-    for load in loads[2:]:
-        load.wait()
+
+    def new_write(k):
+        return pltpu.make_async_copy(new.at[k], new_hbm.at[k], ns.at[k])
+
+    def adj_write(k):
+        return pltpu.make_async_copy(adj.at[k], adj_hbm.at[k], ads.at[k])
 
     def local_group(g, run):
         at = [g * LOCAL_GROUP + i for i in range(LOCAL_GROUP)]
@@ -224,17 +244,42 @@
             sums[j] = run
         return run
 
-    lax.fori_loop(
-        0, slots // LOCAL_GROUP, local_group, jnp.zeros((width, width), jnp.float32)
-    )
-
     def local_row(k, carry):
         used = jnp.where(index[4, k] > 0, 1.0, 0.0)
         total = sums[jnp.maximum(index[3, k], 0)] * used
         base[k] = coup[k].astype(jnp.float32) - total
         return carry
 
-    lax.fori_loop(0, rows, local_row, 0)
+    def finish_row(j, carry):
+        for d in range(1, HIGH):
+            high_copy(d, j).wait_recv()
+        total = own[j, hi].astype(jnp.float32)
+        for d in range(1, HIGH):
+            total += got_high[d - 1, j].astype(jnp.float32)
+        total = base[j] - total
+        new[j] = total
+        new_write(j).start()
+        matrix_high[j], matrix_low[j] = split(
+            three_products(split(diag[j]), split(total), ((1,), (0,)))
+        )
+        return carry
+
+    def solve_row(m, carry):
+        chain_copy(m, sec).wait_recv()
+        adj[m] -= three_products(
+            split(later[m]), (matrix_high[m], matrix_low[m]), ((1,), (1,))
+        )
+
+        @pl.when(sec > 0)
+        def _():
+            chain_copy(m, sec - 1).start()
+
+        adj_write(m).start()
+        return carry
+
+    def finished(c):
+        return jnp.where(c < LOCAL_STEPS, 0, jnp.clip(c - LAG + 1, 0, rows))
+
 
     def step(c, carry):
         @pl.when(c + DEPTH < rows)
@@ -254,40 +299,45 @@
             for d in range(1, HIGH):
                 high_copy(d, c).start()
 
-        j = c - LAG
-
-        @pl.when((j >= 0) & (j < rows))
-        def _():
-            for d in range(1, HIGH):
-                high_copy(d, j).wait_recv()
-            total = own[j, hi].astype(jnp.float32)
-            for d in range(1, HIGH):
-                total += got_high[d - 1, j].astype(jnp.float32)
-            total = base[j] - total
-            new[j] = total
-            matrix[j] = jnp.dot(
-                diag[j], total, precision=precise, preferred_element_type=jnp.float32
+        @pl.when(c == 0)
+        def _():
+            for load in loads[1:]:
+                load.wait()
+
+        @pl.when(c < rows)
+        def _():
+            adj[c] = three_products(split(seed[c]), split(diag[c]), ((1,), (1,)))
+
+        @pl.when((c < rows) & (sec == sections - 1))
+        def _():
+            chain_copy(c, sec - 1).start()
+            adj_write(c).start()
+
+        @pl.when(c < LOCAL_STEPS)
+        def _():
+            per_step = slots // (LOCAL_STEPS * LOCAL_GROUP)
+            running[...] = lax.fori_loop(
+                c * per_step, (c + 1) * per_step, local_group, running[...]
             )
 
-        m = c - LAG - (sections - 2 - sec)
-
-        @pl.when((sec < sections - 1) & (m >= 0) & (m < rows))
-        def _():
-            chain_copy(m, sec).wait_recv()
-            adj[m] -= lax.dot_general(
-                later[m], matrix[m], (((1,), (1,)), ((), ())),
-                precision=precise, preferred_element_type=jnp.float32,
-            )
-
-            @pl.when(sec > 0)
-            def _():
-                chain_copy(m, sec - 1).start()
+        @pl.when(c == LOCAL_STEPS - 1)
+        def _():
+            lax.fori_loop(0, rows, local_row, 0)
+
+        lax.fori_loop(finished(c - 1), finished(c), finish_row, 0)
+        delay = sections - 2 - sec
+
+        @pl.when(sec < sections - 1)
+        def _():
+            lax.fori_loop(finished(c - 1 - delay), finished(c - delay), solve_row, 0)
 
         return carry
 
     lax.fori_loop(0, rows + LAG + sections - 2, step, 0)
 
     def drain(k, carry):
+        new_write(k).wait()
+        adj_write(k).wait()
         for d in range(1, low):
             low_copy(d, k).wait_send()
         for d in range(1, HIGH):
@@ -343,8 +393,12 @@
             grid=(slots // STEP,),
             in_specs=[whole((1, local_slots)), whole((1, local_slots)),
                       streamed(), streamed(), whole(pivot_inverse.shape)],
-            out_specs=[whole((targets,) + block), whole((8, local_slots))],
-            scratch_shapes=[pltpu.VMEM((targets + 1,) + block, jnp.float32)],
+            out_specs=[pl.BlockSpec(memory_space=pl.ANY), whole((8, local_slots))],
+            scratch_shapes=[
+                pltpu.VMEM((targets + 1,) + block, jnp.float32),
+                pltpu.VMEM((targets,) + block, jnp.bfloat16),
+                pltpu.SemaphoreType.DMA((WRITES,)),
+            ],
         ),
         compiler_params=pltpu.CompilerParams(
             dimension_semantics=("arbitrary",), vmem_limit_bytes=VMEM_LIMIT
@@ -358,7 +412,6 @@
       cross_left, cross_right, pivot_inverse)
 
     part = part.reshape((low, rows, HIGH) + block)
-    vmem = pl.BlockSpec(memory_space=pltpu.VMEM)
     hbm = pl.BlockSpec(memory_space=pl.ANY)
     dma = pltpu.SemaphoreType.DMA
     outs = (
@@ -369,11 +422,14 @@
         functools.partial(exchange_kernel, low, sections),
         out_shape=outs,
         in_specs=[pl.BlockSpec(memory_space=pltpu.SMEM)] + [hbm] * 7,
-        out_specs=(vmem, vmem),
+        out_specs=(hbm, hbm),
         scratch_shapes=[
             pltpu.VMEM((rows, HIGH) + block, jnp.bfloat16),
             pltpu.VMEM((low - 1, rows, HIGH) + block, jnp.bfloat16),
             pltpu.VMEM((HIGH - 1, rows) + block, jnp.bfloat16),
+            pltpu.VMEM((rows,) + block, jnp.float32),
+            pltpu.VMEM((rows,) + block, jnp.bfloat16),
+            pltpu.VMEM((rows,) + block, jnp.bfloat16),
             pltpu.VMEM((rows,) + block, jnp.float32),
             pltpu.VMEM((rows,) + block, jnp.float32),
             pltpu.VMEM((rows,) + block, jnp.float32),
@@ -384,11 +440,14 @@
             pltpu.VMEM(local_left.shape, local_left.dtype),
             pltpu.VMEM(local_right.shape, local_right.dtype),
             pltpu.VMEM((local_slots,) + block, jnp.float32),
+            pltpu.VMEM(block, jnp.float32),
             dma((7,)),
             dma((low - 1, rows)),
             dma((low - 1, rows)),
             dma((HIGH - 1, rows)),
             dma((HIGH - 1, rows)),
+            dma((rows,)),
+            dma((rows,)),
             dma((rows,)),
             dma((rows,)),
         ],
@@ -402,7 +461,7 @@
         out_shape=outs,
         in_specs=[hbm, hbm],
         out_specs=(hbm, hbm),
-        scratch_shapes=[dma((2, 4))],
+        scratch_shapes=[pltpu.VMEM((2, rows) + block, jnp.float32), dma((2, 4)), dma((2, 4))],
         compiler_params=pltpu.CompilerParams(vmem_limit_bytes=VMEM_LIMIT),
         name="results",
     )(*results)

time: 157 us -> 80.4 us (0.51)
  Pallas kernels: 155 us -> 77.8 us
    pallas_call x1, Pallas kernels: 64.7 us -> 2.4 us  [per_device(): pl.pallas_call(results_kernel, out_shape=outs, in_specs=[hbm, hbm], out_s...]
    pallas_call x1, Pallas kernels: 76.1 us -> 63.6 us  [per_device(): pl.pallas_call(functools.partial(exchange_kernel, low, sections), out_sha...]
    pallas_call x1, Pallas kernels: 13.8 us -> 11.8 us  [per_device(): pl.pallas_call(functools.partial(products_kernel, low, rows), out_shape=(...]
where the time goes in v3:
time: 80.4 us; the launch traced here: 79.1 us
  Pallas kernels  77.8 us (97%)
  between operations  1.29 us (2%)
    pallas_call x1, Pallas kernels, per_device(): pl.pallas_call(functools.partial(exchange_kernel, low, sections), out_sha...  63.6 us
    pallas_call x1, Pallas kernels, per_device(): pl.pallas_call(functools.partial(products_kernel, low, rows), out_shape=(...  11.8 us
    pallas_call x1, Pallas kernels, per_device(): pl.pallas_call(results_kernel, out_shape=outs, in_specs=[hbm, hbm], out_s...  2.4 us

profile of v3, /device:TPU:1, one launch (start us, length us, event | category | flops | bytes accessed | tf_op | source)
XLA Modules:
  0.0 79.1 jit_solution(11999207947290388959)
XLA Ops:
  1.3 11.8 %products.1 = (bf16[128,128,128]{2,1,0:T(8,128)(2,1)}, s32[8,128]{1,0:T(8,128)}) custom-call(s32[128]{0:T(128)} %cpiv.1, s32[128]{0:T(128)} %bitcast.5, s32[128]{0:T(128)} %crow.1, s32[1]{0:T(128)S(6)} %copy.16.ccount, s32[1,128]{1,0:T(1,128)} %bitcast.6, s32[1,128]{1,0:T(1,128)} %bitcast.7, bf16[128,128,128]{2,1,0:T(8,128)(2,1)} %cl.1, ...), custom_call_target="tpu_custom_call" | custom-call | flops 1073741824 | bytes 12582912 | tf_op jit(solution)/shard_map/products/pallas_call | solution.py:385
  13.1 63.6 %exchange.1 = (f32[16,128,128]{2,1,0:T(8,128)}, f32[16,128,128]{2,1,0:T(8,128)}) custom-call(s32[8,128]{1,0:T(8,128)} %get-tuple-element.6.index, bf16[2,16,4,128,128]{4,3,2,1,0:T(8,128)(2,1)} %bitcast.4, bf16[16,128,128]{2,1,0:T(8,128)(2,1)} %coup_hbm.1, f32[16,128,128]{2,1,0:T(8,128)} %diag_hbm.1, f32[16,128,128]{2,1,0:T(8,128)} %seed_hbm.1, ...), custom_call_target="tpu_custom_call" | custom-call | tf_op jit(solution)/shard_map/exchange/pallas_call | solution.py:421
  76.7 2.4 %results.1 = (f32[16,128,128]{2,1,0:T(8,128)}, f32[16,128,128]{2,1,0:T(8,128)}) custom-call(f32[16,128,128]{2,1,0:T(8,128)} %get-tuple-element.8.new_in, f32[16,128,128]{2,1,0:T(8,128)} %get-tuple-element.9.adj_in), custom_call_target="tpu_custom_call" | custom-call | tf_op jit(solution)/shard_map/results/pallas_call | solution.py:459

commit v4 on v3

v4 whole, which is shorter than its diff:
```python
import functools

import jax
import jax.numpy as jnp
from jax import lax
from jax.experimental import pallas as pl
from jax.experimental.pallas import tpu as pltpu
from jax.sharding import PartitionSpec as P

GROUP = 4
DEPTH = 4
HIGH = 4
LAG = 2
LOCAL_STEPS = 4
CAP = 16
FIRST_PIECES = 4
LANES = 128
VMEM_LIMIT = 56 * 1024 * 1024
MESH = pl.DeviceIdType.MESH


def order_kernel(low, rows, ccount, cpiv, cown, crow, lpiv, lrow, index):
    n = cpiv.shape[1]
    row = lax.axis_index("row")
    hi, lo = row // low, row % low
    lane = lax.broadcasted_iota(jnp.int32, (n, n), 1).astype(jnp.float32)
    slot = lax.broadcasted_iota(jnp.int32, (n, n), 0).astype(jnp.float32)

    def down(x):
        return jnp.broadcast_to(x, (n, n)).T

    def total(x):
        return jnp.sum(x, axis=0, keepdims=True)

    def put(at, x):
        index[at:at + 1, :] = x.astype(jnp.int32)

    def sort(at, key, pivot):
        key_down = down(key)
        spread = key * n + lane[:1]
        rank = total(jnp.where(down(spread) < spread, 1.0, 0.0))
        hit = down(rank) == lane
        put(at, total(jnp.where(hit, slot, 0.0)))
        put(at + 1, total(jnp.where(hit, down(pivot), 0.0)))
        put(at + 2, total(jnp.where(hit, key_down, 0.0)))
        return key_down

    def ends(at, at_count, key_down, first):
        put(at, total(jnp.where(key_down <= lane + first, 1.0, 0.0)) - 1.0)
        put(at_count, total(jnp.where(key_down == lane + first, 1.0, 0.0)))

    local_down = sort(0, lrow[...].astype(jnp.float32), lpiv[...].astype(jnp.float32))
    ends(3, 4, local_down, 0.0)
    owner = cown[...]
    far = ((owner // low) - hi - 1) & (HIGH - 1)
    near = ((owner & (low - 1)) - lo - 1) & (low - 1)
    key = (far * low + near) * rows + crow[...]
    slot_number = lax.broadcasted_iota(jnp.int32, (1, n), 1)
    targets = HIGH * low * rows
    key = jnp.where(slot_number < ccount[0], key, targets)
    cross_down = sort(5, key.astype(jnp.float32), cpiv[...].astype(jnp.float32))
    for p in range(targets // n):
        ends(8 + p, 12 + p, cross_down, float(p * n))


def results_kernel(new_in, adj_in, new_out, adj_out, held, in_sems, out_sems):
    pieces = in_sems.shape[1]
    size = new_in.shape[0] // pieces
    reads, writes = [], []
    for a, (source, target) in enumerate(((new_in, new_out), (adj_in, adj_out))):
        for p in range(pieces):
            span = pl.ds(p * size, size)
            reads.append(
                pltpu.make_async_copy(source.at[span], held.at[a, span], in_sems.at[a, p])
            )
            writes.append(
                pltpu.make_async_copy(held.at[a, span], target.at[span], out_sems.at[a, p])
            )
    for read in reads:
        read.start()
    for read, write in zip(reads, writes):
        read.wait()
        write.start()
    for write in writes:
        write.wait()


def split(x):
    high = x.astype(jnp.bfloat16)
    return high, (x - high.astype(jnp.float32)).astype(jnp.bfloat16)


def three_products(left, right, contract):
    def one(a, b):
        return lax.dot_general(a, b, (contract, ((), ())), preferred_element_type=jnp.float32)

    return one(left[0], right[0]) + (one(left[0], right[1]) + one(left[1], right[0]))


def exchange_kernel(
    low, sections, index, cleft_hbm, cright_hbm, coup_hbm, diag_hbm, seed_hbm, pinv_hbm,
    left_hbm, right_hbm,
    new_hbm, adj_hbm,
    part, got_low, got_high, later, matrix_high, matrix_low, new, adj,
    base, coup, diag, seed, pinv, cleft, cright, left, right, sums, running,
    load_sem, fs, fr, ls, lr, hs, hr, vs, vr, ns, ads,
):
    rows, width, _ = base.shape
    slots = left.shape[0]
    row = lax.axis_index("row")
    sec = lax.axis_index("section")
    hi, lo = row // low, row % low

    loads = [
        pltpu.make_async_copy(source, target, load_sem.at[i])
        for i, (source, target) in enumerate((
            (pinv_hbm, pinv), (cleft_hbm, cleft), (cright_hbm, cright), (seed_hbm, seed),
            (diag_hbm, diag), (left_hbm, left), (right_hbm, right), (coup_hbm, coup),
        ))
    ]
    for load in loads:
        load.start()
    running[...] = jnp.zeros_like(running)

    barrier = pltpu.get_barrier_semaphore()
    for d in range(1, low):
        peer = hi * low + (lo + d) % low
        pl.semaphore_signal(barrier, inc=1, device_id={"row": peer}, device_id_type=MESH)
    for d in range(1, HIGH):
        peer = ((hi + d) % HIGH) * low + lo
        pl.semaphore_signal(barrier, inc=1, device_id={"row": peer}, device_id_type=MESH)

    @pl.when(sec > 0)
    def _():
        pl.semaphore_signal(
            barrier, inc=1, device_id={"section": sec - 1}, device_id_type=MESH
        )

    @pl.when(sec < sections - 1)
    def _():
        pl.semaphore_signal(
            barrier, inc=1, device_id={"section": sec + 1}, device_id_type=MESH
        )

    ends = jnp.where(sec > 0, 1, 0) + jnp.where(sec < sections - 1, 1, 0)
    pl.semaphore_wait(barrier, (low - 1) + (HIGH - 1) + ends)

    own = low - 1
    piece = rows // FIRST_PIECES

    def low_transfer(d, span, far, send_sem, recv_sem):
        return pltpu.make_async_remote_copy(
            src_ref=part.at[d - 1, span, far],
            dst_ref=got_low.at[d - 1, span, far],
            send_sem=send_sem,
            recv_sem=recv_sem,
            device_id={"row": hi * low + (lo + d) % low},
            device_id_type=MESH,
        )

    def first_copy(d, r):
        return low_transfer(d, pl.ds(r * piece, piece), 0, fs.at[d - 1, r], fr.at[d - 1, r])

    def low_copy(d, k):
        return low_transfer(d, k, pl.ds(1, HIGH - 1), ls.at[d - 1, k], lr.at[d - 1, k])

    def high_copy(d, k):
        return pltpu.make_async_remote_copy(
            src_ref=part.at[own, k, d - 1],
            dst_ref=got_high.at[d - 1, k],
            send_sem=hs.at[d - 1, k],
            recv_sem=hr.at[d - 1, k],
            device_id={"row": ((hi + d) % HIGH) * low + lo},
            device_id_type=MESH,
        )

    def merge(k, far):
        total = part[own, k, far].astype(jnp.float32)
        for d in range(1, low):
            total += got_low[d - 1, k, far].astype(jnp.float32)
        part[own, k, far] = total.astype(part.dtype)

    def chain_copy(k, target):
        return pltpu.make_async_remote_copy(
            src_ref=adj.at[k],
            dst_ref=later.at[k],
            send_sem=vs.at[k],
            recv_sem=vr.at[k],
            device_id={"section": target},
            device_id_type=MESH,
        )

    def products(at, pivots, order, first, second, run):
        scaled = [
            jnp.dot(
                first[index[order, j]], pinv[index[pivots, j]],
                preferred_element_type=jnp.float32,
            ).astype(jnp.bfloat16)
            for j in at
        ]
        updates = [
            jnp.dot(half, second[index[order, j]], preferred_element_type=jnp.float32)
            for half, j in zip(scaled, at)
        ]
        for update, j in zip(updates, at):
            same = index[order + 2, j] == index[order + 2, jnp.maximum(j - 1, 0)]
            run = run * jnp.where(same, 1.0, 0.0) + update
            sums[j] = run
        return run

    for load in loads[:3]:
        load.wait()

    def owner_group(q, run):
        far, near = q // low, q % low
        for p in range(CAP // GROUP):
            at = [q * CAP + p * GROUP + i for i in range(GROUP)]
            run = products(at, 6, 5, cleft, cright, run)
        for k in range(rows):
            spot = q * rows + k
            line, place = spot // LANES, spot % LANES
            used = jnp.where(index[12 + line, place] > 0, 1.0, 0.0)
            total = sums[jnp.maximum(index[8 + line, place], 0)] * used
            part[near, k, far] = total.astype(part.dtype)
        for d in range(1, low):

            @pl.when(q == d - 1)
            def _():
                for r in range(FIRST_PIECES):
                    first_copy(d, r).start()

        return run

    def owner_group_and_merge(q, run):
        run = owner_group(q, run)
        r = q - (HIGH * low - FIRST_PIECES)
        for d in range(1, low):
            first_copy(d, r).wait_recv()
        for i in range(piece):
            merge(r * piece + i, 0)
            high_copy(1, r * piece + i).start()
        return run

    plain = HIGH * low - FIRST_PIECES
    run = lax.fori_loop(0, plain, owner_group, jnp.zeros((width, width), jnp.float32))
    lax.fori_loop(plain, HIGH * low, owner_group_and_merge, run)

    for k in range(DEPTH):
        for d in range(1, low):
            low_copy(d, k).start()

    def new_write(k):
        return pltpu.make_async_copy(new.at[k], new_hbm.at[k], ns.at[k])

    def adj_write(k):
        return pltpu.make_async_copy(adj.at[k], adj_hbm.at[k], ads.at[k])

    def local_group(g, run):
        at = [g * GROUP + i for i in range(GROUP)]
        return products(at, 1, 0, left, right, run)

    def local_row(k, carry):
        used = jnp.where(index[4, k] > 0, 1.0, 0.0)
        total = sums[jnp.maximum(index[3, k], 0)] * used
        base[k] = coup[k].astype(jnp.float32) - total
        return carry

    def finish_row(j, carry):
        for d in range(1, HIGH):
            high_copy(d, j).wait_recv()
        total = part[own, j, HIGH - 1].astype(jnp.float32)
        for d in range(1, HIGH):
            total += got_high[d - 1, j].astype(jnp.float32)
        total = base[j] - total
        new[j] = total
        new_write(j).start()
        matrix_high[j], matrix_low[j] = split(
            three_products(split(diag[j]), split(total), ((1,), (0,)))
        )
        return carry

    def solve_row(m, carry):
        chain_copy(m, sec).wait_recv()
        adj[m] -= three_products(
            split(later[m]), (matrix_high[m], matrix_low[m]), ((1,), (1,))
        )

        @pl.when(sec > 0)
        def _():
            chain_copy(m, sec - 1).start()

        adj_write(m).start()
        return carry

    def finished(c):
        return jnp.where(c < LOCAL_STEPS, 0, jnp.clip(c - LAG + 1, 0, rows))


    def step(c, carry):
        @pl.when(c + DEPTH < rows)
        def _():
            for d in range(1, low):
                low_copy(d, c + DEPTH).start()

        @pl.when(c < rows)
        def _():
            for d in range(1, low):
                low_copy(d, c).wait_recv()
            for far in range(1, HIGH):
                merge(c, far)
                if far < HIGH - 1:
                    high_copy(far + 1, c).start()

        @pl.when(c == 0)
        def _():
            for load in loads[3:]:
                load.wait()

        @pl.when(c < rows)
        def _():
            adj[c] = three_products(split(seed[c]), split(diag[c]), ((1,), (1,)))

        @pl.when((c < rows) & (sec == sections - 1))
        def _():
            chain_copy(c, sec - 1).start()
            adj_write(c).start()

        @pl.when(c < LOCAL_STEPS)
        def _():
            per_step = slots // (LOCAL_STEPS * GROUP)
            running[...] = lax.fori_loop(
                c * per_step, (c + 1) * per_step, local_group, running[...]
            )

        @pl.when(c == LOCAL_STEPS - 1)
        def _():
            lax.fori_loop(0, rows, local_row, 0)

        lax.fori_loop(finished(c - 1), finished(c), finish_row, 0)
        delay = sections - 2 - sec

        @pl.when(sec < sections - 1)
        def _():
            lax.fori_loop(finished(c - 1 - delay), finished(c - delay), solve_row, 0)

        return carry

    lax.fori_loop(0, rows + LAG + sections - 2, step, 0)

    def drain(k, carry):
        new_write(k).wait()
        adj_write(k).wait()
        for d in range(1, low):
            low_copy(d, k).wait_send()
        for d in range(1, HIGH):
            high_copy(d, k).wait_send()

        @pl.when(sec > 0)
        def _():
            chain_copy(k, sec - 1).wait_send()

        return carry

    lax.fori_loop(0, rows, drain, 0)
    for r in range(FIRST_PIECES):
        for d in range(1, low):
            first_copy(d, r).wait_send()


def per_device(
    coupling,
    diag_inverse,
    pivot_inverse,
    cross_left,
    cross_right,
    cross_pivot,
    cross_owner,
    foreign_target_row,
    cross_count,
    local_left,
    local_right,
    local_pivot,
    local_target,
    adjoint_seed,
):
    rows, width, _ = coupling.shape
    groups = lax.axis_size("row")
    sections = lax.axis_size("section")
    low = groups // HIGH
    slots, local_slots = cross_left.shape[0], local_left.shape[0]
    block = (width, width)
    scalars = pl.BlockSpec(memory_space=pltpu.SMEM)
    vector = pl.BlockSpec(memory_space=pltpu.VMEM)

    def flat(x):
        return x.reshape(1, x.size)

    index = pl.pallas_call(
        functools.partial(order_kernel, low, rows),
        out_shape=jax.ShapeDtypeStruct((16, slots), jnp.int32),
        in_specs=[scalars] + [vector] * 5,
        out_specs=vector,
        name="order",
    )(cross_count, flat(cross_pivot), flat(cross_owner), flat(foreign_target_row),
      flat(local_pivot), flat(local_target))

    hbm = pl.BlockSpec(memory_space=pl.ANY)
    dma = pltpu.SemaphoreType.DMA
    outs = (
        jax.ShapeDtypeStruct((rows,) + block, jnp.float32),
        jax.ShapeDtypeStruct((rows,) + block, jnp.float32),
    )
    results = pl.pallas_call(
        functools.partial(exchange_kernel, low, sections),
        out_shape=outs,
        in_specs=[scalars] + [hbm] * 8,
        out_specs=(hbm, hbm),
        scratch_shapes=[
            pltpu.VMEM((low, rows, HIGH) + block, jnp.bfloat16),
            pltpu.VMEM((low - 1, rows, HIGH) + block, jnp.bfloat16),
            pltpu.VMEM((HIGH - 1, rows) + block, jnp.bfloat16),
            pltpu.VMEM((rows,) + block, jnp.float32),
            pltpu.VMEM((rows,) + block, jnp.bfloat16),
            pltpu.VMEM((rows,) + block, jnp.bfloat16),
            pltpu.VMEM((rows,) + block, jnp.float32),
            pltpu.VMEM((rows,) + block, jnp.float32),
            pltpu.VMEM((rows,) + block, jnp.float32),
            pltpu.VMEM(coupling.shape, coupling.dtype),
            pltpu.VMEM(diag_inverse.shape, jnp.float32),
            pltpu.VMEM(adjoint_seed.shape, jnp.float32),
            pltpu.VMEM(pivot_inverse.shape, pivot_inverse.dtype),
            pltpu.VMEM(cross_left.shape, cross_left.dtype),
            pltpu.VMEM(cross_right.shape, cross_right.dtype),
            pltpu.VMEM(local_left.shape, local_left.dtype),
            pltpu.VMEM(local_right.shape, local_right.dtype),
            pltpu.VMEM((local_slots,) + block, jnp.float32),
            pltpu.VMEM(block, jnp.float32),
            dma((8,)),
            dma((low - 1, FIRST_PIECES)),
            dma((low - 1, FIRST_PIECES)),
            dma((low - 1, rows)),
            dma((low - 1, rows)),
            dma((HIGH - 1, rows)),
            dma((HIGH - 1, rows)),
            dma((rows,)),
            dma((rows,)),
            dma((rows,)),
            dma((rows,)),
        ],
        compiler_params=pltpu.CompilerParams(
            collective_id=0, has_side_effects=True, vmem_limit_bytes=VMEM_LIMIT
        ),
        name="exchange",
    )(index, cross_left, cross_right, coupling, diag_inverse, adjoint_seed, pivot_inverse,
      local_left, local_right)
    return pl.pallas_call(
        results_kernel,
        out_shape=outs,
        in_specs=[hbm, hbm],
        out_specs=(hbm, hbm),
        scratch_shapes=[pltpu.VMEM((2, rows) + block, jnp.float32), dma((2, 4)), dma((2, 4))],
        compiler_params=pltpu.CompilerParams(vmem_limit_bytes=VMEM_LIMIT),
        name="results",
    )(*results)


def solution(mesh):
    spread = P(("section", "row"))
    return jax.shard_map(
        per_device,
        mesh=mesh,
        in_specs=(spread,) * 14,
        out_specs=(spread, spread),
        check_vma=False,
    )
```

time: 80.4 us -> 76.3 us (0.949)
  Pallas kernels: 77.8 us -> 73.6 us
    pallas_call x1, Pallas kernels: 11.8 us -> 1.58 us  [per_device(): pl.pallas_call(functools.partial(order_kernel, low, rows), out_shape=jax....]
    pallas_call x1, Pallas kernels: 63.6 us -> 69.6 us  [per_device(): pl.pallas_call(functools.partial(exchange_kernel, low, sections), out_sha...]
where the time goes in v4:
time: 76.3 us; the launch traced here: 74.9 us
  Pallas kernels  73.6 us (96%)
  between operations  1.29 us (2%)
    pallas_call x1, Pallas kernels, per_device(): pl.pallas_call(functools.partial(exchange_kernel, low, sections), out_sha...  69.6 us
    pallas_call x1, Pallas kernels, per_device(): pl.pallas_call(results_kernel, out_shape=outs, in_specs=[hbm, hbm], out_s...  2.4 us
    pallas_call x1, Pallas kernels, per_device(): pl.pallas_call(functools.partial(order_kernel, low, rows), out_shape=jax....  1.58 us

profile of v4, /device:TPU:1, one launch (start us, length us, event | category | flops | bytes accessed | tf_op | source)
XLA Modules:
  0.0 74.9 jit_solution(7241154761616133513)
XLA Ops:
  1.3 1.6 %order.1.index = s32[16,128]{1,0:T(8,128)} custom-call(s32[1]{0:T(128)S(6)} %copy.16.ccount, s32[1,128]{1,0:T(1,128)} %bitcast.5, s32[1,128]{1,0:T(1,128)} %bitcast.6, s32[1,128]{1,0:T(1,128)} %bitcast.7, s32[1,128]{1,0:T(1,128)} %bitcast.8, s32[1,128]{1,0:T(1,128)} %bitcast.9), custom_call_target="tpu_custom_call" | custom-call | tf_op jit(solution)/shard_map/order/pallas_call | solution.py:398
  2.9 69.6 %exchange.1 = (f32[16,128,128]{2,1,0:T(8,128)}, f32[16,128,128]{2,1,0:T(8,128)}) custom-call(s32[16,128]{1,0:T(8,128)} %order.1.index, bf16[128,128,128]{2,1,0:T(8,128)(2,1)} %cleft_hbm.1, bf16[128,128,128]{2,1,0:T(8,128)(2,1)} %cright_hbm.1, bf16[16,128,128]{2,1,0:T(8,128)(2,1)} %coup_hbm.1, f32[16,128,128]{2,1,0:T(8,128)} %diag_hbm.1, ...), custom_call_target="tpu_custom_call" | custom-call | tf_op jit(solution)/shard_map/exchange/pallas_call | solution.py:413
  72.5 2.4 %results.1 = (f32[16,128,128]{2,1,0:T(8,128)}, f32[16,128,128]{2,1,0:T(8,128)}) custom-call(f32[16,128,128]{2,1,0:T(8,128)} %get-tuple-element.4.new_in, f32[16,128,128]{2,1,0:T(8,128)} %get-tuple-element.5.adj_in), custom_call_target="tpu_custom_call" | custom-call | tf_op jit(solution)/shard_map/results/pallas_call | solution.py:456

commit v5 on v4

--- a/solution.py
+++ b/solution.py
@@ -7,10 +7,10 @@
 from jax.experimental.pallas import tpu as pltpu
 from jax.sharding import PartitionSpec as P
 
-GROUP = 4
+GROUP = 8
 DEPTH = 4
 HIGH = 4
-LAG = 2
+LAG = 3
 LOCAL_STEPS = 4
 CAP = 16
 FIRST_PIECES = 4
@@ -101,9 +101,9 @@
     low, sections, index, cleft_hbm, cright_hbm, coup_hbm, diag_hbm, seed_hbm, pinv_hbm,
     left_hbm, right_hbm,
     new_hbm, adj_hbm,
-    part, got_low, got_high, later, matrix_high, matrix_low, new, adj,
+    part, got_low, got_high, relayed, later, matrix_high, matrix_low, new, adj,
     base, coup, diag, seed, pinv, cleft, cright, left, right, sums, running,
-    load_sem, fs, fr, ls, lr, hs, hr, vs, vr, ns, ads,
+    load_sem, fs, fr, ls, lr, hs, hr, rs, rr, vs, vr, ns, ads,
 ):
     rows, width, _ = base.shape
     slots = left.shape[0]
@@ -122,6 +122,15 @@
         load.start()
     running[...] = jnp.zeros_like(running)
 
+    @pl.when(hi == 0)
+    def _():
+        got_high[0] = jnp.zeros(got_high.shape[1:], got_high.dtype)
+
+    @pl.when(hi == HIGH - 1)
+    def _():
+        got_high[HIGH - 2] = jnp.zeros(got_high.shape[1:], got_high.dtype)
+
+
     barrier = pltpu.get_barrier_semaphore()
     for d in range(1, low):
         peer = hi * low + (lo + d) % low
@@ -173,6 +182,44 @@
             device_id={"row": ((hi + d) % HIGH) * low + lo},
             device_id_type=MESH,
         )
+
+    edge = (hi == 0) | (hi == HIGH - 1)
+
+    def relay_copy(k):
+        return pltpu.make_async_remote_copy(
+            src_ref=part.at[own, k, jnp.where(hi == 0, HIGH - 2, 0)],
+            dst_ref=relayed.at[k],
+            send_sem=rs.at[k],
+            recv_sem=rr.at[k],
+            device_id={"row": jnp.where(hi == 0, 1, HIGH - 2) * low + lo},
+            device_id_type=MESH,
+        )
+
+    def sends_far(d):
+        return {1: hi == HIGH - 1, HIGH - 1: hi == 0}.get(d)
+
+    def gets_none(d):
+        return {1: hi == 0, HIGH - 1: hi == HIGH - 1}.get(d)
+
+    def unless(condition, act):
+        if condition is None:
+            act()
+        else:
+            pl.when(jnp.logical_not(condition))(act)
+
+    def send_high(d, k):
+        unless(sends_far(d), lambda: high_copy(d, k).start())
+        if sends_far(d) is not None:
+            pl.when(sends_far(d))(lambda: relay_copy(k).start())
+
+    def send_middle(k):
+        @pl.when(jnp.logical_not(edge))
+        def _():
+            relay_copy(k).wait_recv()
+            total = part[own, k, 1].astype(jnp.float32) + relayed[k].astype(jnp.float32)
+            part[own, k, 1] = total.astype(part.dtype)
+
+        send_high(2, k)
 
     def merge(k, far):
         total = part[own, k, far].astype(jnp.float32)
@@ -238,7 +285,7 @@
             first_copy(d, r).wait_recv()
         for i in range(piece):
             merge(r * piece + i, 0)
-            high_copy(1, r * piece + i).start()
+            send_high(1, r * piece + i)
         return run
 
     plain = HIGH * low - FIRST_PIECES
@@ -267,7 +314,7 @@
 
     def finish_row(j, carry):
         for d in range(1, HIGH):
-            high_copy(d, j).wait_recv()
+            unless(gets_none(d), lambda d=d: high_copy(d, j).wait_recv())
         total = part[own, j, HIGH - 1].astype(jnp.float32)
         for d in range(1, HIGH):
             total += got_high[d - 1, j].astype(jnp.float32)
@@ -308,8 +355,12 @@
                 low_copy(d, c).wait_recv()
             for far in range(1, HIGH):
                 merge(c, far)
-                if far < HIGH - 1:
-                    high_copy(far + 1, c).start()
+                if far == HIGH - 2:
+                    send_high(HIGH - 1, c)
+
+        @pl.when((c >= 1) & (c <= rows))
+        def _():
+            send_middle(c - 1)
 
         @pl.when(c == 0)
         def _():
@@ -353,7 +404,11 @@
         for d in range(1, low):
             low_copy(d, k).wait_send()
         for d in range(1, HIGH):
-            high_copy(d, k).wait_send()
+            unless(sends_far(d), lambda d=d: high_copy(d, k).wait_send())
+
+        @pl.when(edge)
+        def _():
+            relay_copy(k).wait_send()
 
         @pl.when(sec > 0)
         def _():
@@ -419,6 +474,7 @@
             pltpu.VMEM((low, rows, HIGH) + block, jnp.bfloat16),
             pltpu.VMEM((low - 1, rows, HIGH) + block, jnp.bfloat16),
             pltpu.VMEM((HIGH - 1, rows) + block, jnp.bfloat16),
+            pltpu.VMEM((rows,) + block, jnp.bfloat16),
             pltpu.VMEM((rows,) + block, jnp.float32),
             pltpu.VMEM((rows,) + block, jnp.bfloat16),
             pltpu.VMEM((rows,) + block, jnp.bfloat16),
@@ -446,6 +502,8 @@
             dma((rows,)),
             dma((rows,)),
             dma((rows,)),
+            dma((rows,)),
+            dma((rows,)),
         ],
         compiler_params=pltpu.CompilerParams(
             collective_id=0, has_side_effects=True, vmem_limit_bytes=VMEM_LIMIT

time: 76.3 us -> 75 us (0.983)
  Pallas kernels: 73.6 us -> 72.4 us
    pallas_call x1, Pallas kernels: 69.6 us -> 68.4 us  [per_device(): pl.pallas_call(functools.partial(exchange_kernel, low, sections), out_sha...]
where the time goes in v5:
time: 75 us; the launch traced here: 73.7 us
  Pallas kernels  72.4 us (97%)
  between operations  1.29 us (2%)
    pallas_call x1, Pallas kernels, per_device(): pl.pallas_call(functools.partial(exchange_kernel, low, sections), out_sha...  68.4 us
    pallas_call x1, Pallas kernels, per_device(): pl.pallas_call(results_kernel, out_shape=outs, in_specs=[hbm, hbm], out_s...  2.4 us
    pallas_call x1, Pallas kernels, per_device(): pl.pallas_call(functools.partial(order_kernel, low, rows), out_shape=jax....  1.58 us

profile of v5, /device:TPU:1, one launch (start us, length us, event | category | flops | bytes accessed | tf_op | source)
XLA Modules:
  0.0 73.7 jit_solution(8461131448493278960)
XLA Ops:
  1.3 1.6 %order.1.index = s32[16,128]{1,0:T(8,128)} custom-call(s32[1]{0:T(128)S(6)} %copy.16.ccount, s32[1,128]{1,0:T(1,128)} %bitcast.5, s32[1,128]{1,0:T(1,128)} %bitcast.6, s32[1,128]{1,0:T(1,128)} %bitcast.7, s32[1,128]{1,0:T(1,128)} %bitcast.8, s32[1,128]{1,0:T(1,128)} %bitcast.9), custom_call_target="tpu_custom_call" | custom-call | tf_op jit(solution)/shard_map/order/pallas_call | solution.py:453
  2.9 68.4 %exchange.1 = (f32[16,128,128]{2,1,0:T(8,128)}, f32[16,128,128]{2,1,0:T(8,128)}) custom-call(s32[16,128]{1,0:T(8,128)} %order.1.index, bf16[128,128,128]{2,1,0:T(8,128)(2,1)} %cleft_hbm.1, bf16[128,128,128]{2,1,0:T(8,128)(2,1)} %cright_hbm.1, bf16[16,128,128]{2,1,0:T(8,128)(2,1)} %coup_hbm.1, f32[16,128,128]{2,1,0:T(8,128)} %diag_hbm.1, ...), custom_call_target="tpu_custom_call" | custom-call | tf_op jit(solution)/shard_map/exchange/pallas_call | solution.py:468
  71.3 2.4 %results.1 = (f32[16,128,128]{2,1,0:T(8,128)}, f32[16,128,128]{2,1,0:T(8,128)}) custom-call(f32[16,128,128]{2,1,0:T(8,128)} %get-tuple-element.4.new_in, f32[16,128,128]{2,1,0:T(8,128)} %get-tuple-element.5.adj_in), custom_call_target="tpu_custom_call" | custom-call | tf_op jit(solution)/shard_map/results/pallas_call | solution.py:514

commit v6 on v5

--- a/solution.py
+++ b/solution.py
@@ -54,7 +54,7 @@
     owner = cown[...]
     far = ((owner // low) - hi - 1) & (HIGH - 1)
     near = ((owner & (low - 1)) - lo - 1) & (low - 1)
-    key = (far * low + near) * rows + crow[...]
+    key = (near * HIGH + far) * rows + crow[...]
     slot_number = lax.broadcasted_iota(jnp.int32, (1, n), 1)
     targets = HIGH * low * rows
     key = jnp.where(slot_number < ccount[0], key, targets)
@@ -259,7 +259,7 @@
         load.wait()
 
     def owner_group(q, run):
-        far, near = q // low, q % low
+        far, near = q % HIGH, q // HIGH
         for p in range(CAP // GROUP):
             at = [q * CAP + p * GROUP + i for i in range(GROUP)]
             run = products(at, 6, 5, cleft, cright, run)
@@ -271,10 +271,16 @@
             part[near, k, far] = total.astype(part.dtype)
         for d in range(1, low):
 
-            @pl.when(q == d - 1)
+            @pl.when(q == (d - 1) * HIGH)
             def _():
                 for r in range(FIRST_PIECES):
                     first_copy(d, r).start()
+
+        @pl.when(q == own * HIGH - 1)
+        def _():
+            for k in range(DEPTH):
+                for d in range(1, low):
+                    low_copy(d, k).start()
 
         return run
 
@@ -291,10 +297,6 @@
     plain = HIGH * low - FIRST_PIECES
     run = lax.fori_loop(0, plain, owner_group, jnp.zeros((width, width), jnp.float32))
     lax.fori_loop(plain, HIGH * low, owner_group_and_merge, run)
-
-    for k in range(DEPTH):
-        for d in range(1, low):
-            low_copy(d, k).start()
 
     def new_write(k):
         return pltpu.make_async_copy(new.at[k], new_hbm.at[k], ns.at[k])
@@ -340,7 +342,8 @@
         return carry
 
     def finished(c):
-        return jnp.where(c < LOCAL_STEPS, 0, jnp.clip(c - LAG + 1, 0, rows))
+        done = jnp.where(c < rows, jnp.clip(c - LAG + 1, 0, rows), rows)
+        return jnp.where(c < LOCAL_STEPS, 0, done)
 
 
     def step(c, carry):
@@ -396,7 +399,7 @@
 
         return carry
 
-    lax.fori_loop(0, rows + LAG + sections - 2, step, 0)
+    lax.fori_loop(0, rows + sections - 1, step, 0)
 
     def drain(k, carry):
         new_write(k).wait()

time: 75 us -> 76 us (1.013)
  Pallas kernels: 72.4 us -> 73.3 us
    pallas_call x1, Pallas kernels: 68.4 us -> 69.3 us  [per_device(): pl.pallas_call(functools.partial(exchange_kernel, low, sections), out_sha...]
where the time goes in v6:
time: 76 us; the launch traced here: 74.6 us
  Pallas kernels  73.3 us (96%)
  between operations  1.29 us (2%)
    pallas_call x1, Pallas kernels, per_device(): pl.pallas_call(functools.partial(exchange_kernel, low, sections), out_sha...  69.3 us
    pallas_call x1, Pallas kernels, per_device(): pl.pallas_call(results_kernel, out_shape=outs, in_specs=[hbm, hbm], out_s...  2.4 us
    pallas_call x1, Pallas kernels, per_device(): pl.pallas_call(functools.partial(order_kernel, low, rows), out_shape=jax....  1.58 us

profile of v6, /device:TPU:1, one launch (start us, length us, event | category | flops | bytes accessed | tf_op | source)
XLA Modules:
  0.0 74.6 jit_solution(8474006048534524788)
XLA Ops:
  1.3 1.6 %order.1.index = s32[16,128]{1,0:T(8,128)} custom-call(s32[1]{0:T(128)S(6)} %copy.16.ccount, s32[1,128]{1,0:T(1,128)} %bitcast.5, s32[1,128]{1,0:T(1,128)} %bitcast.6, s32[1,128]{1,0:T(1,128)} %bitcast.7, s32[1,128]{1,0:T(1,128)} %bitcast.8, s32[1,128]{1,0:T(1,128)} %bitcast.9), custom_call_target="tpu_custom_call" | custom-call | tf_op jit(solution)/shard_map/order/pallas_call | solution.py:456
  2.9 69.3 %exchange.1 = (f32[16,128,128]{2,1,0:T(8,128)}, f32[16,128,128]{2,1,0:T(8,128)}) custom-call(s32[16,128]{1,0:T(8,128)} %order.1.index, bf16[128,128,128]{2,1,0:T(8,128)(2,1)} %cleft_hbm.1, bf16[128,128,128]{2,1,0:T(8,128)(2,1)} %cright_hbm.1, bf16[16,128,128]{2,1,0:T(8,128)(2,1)} %coup_hbm.1, f32[16,128,128]{2,1,0:T(8,128)} %diag_hbm.1, ...), custom_call_target="tpu_custom_call" | custom-call | tf_op jit(solution)/shard_map/exchange/pallas_call | solution.py:471
  72.2 2.4 %results.1 = (f32[16,128,128]{2,1,0:T(8,128)}, f32[16,128,128]{2,1,0:T(8,128)}) custom-call(f32[16,128,128]{2,1,0:T(8,128)} %get-tuple-element.4.new_in, f32[16,128,128]{2,1,0:T(8,128)} %get-tuple-element.5.adj_in), custom_call_target="tpu_custom_call" | custom-call | tf_op jit(solution)/shard_map/results/pallas_call | solution.py:517

commit v7 on v5

--- a/solution.py
+++ b/solution.py
@@ -11,7 +11,7 @@
 DEPTH = 4
 HIGH = 4
 LAG = 3
-LOCAL_STEPS = 4
+LOCAL_STEPS = 8
 CAP = 16
 FIRST_PIECES = 4
 LANES = 128
@@ -340,7 +340,8 @@
         return carry
 
     def finished(c):
-        return jnp.where(c < LOCAL_STEPS, 0, jnp.clip(c - LAG + 1, 0, rows))
+        done = jnp.where(c < rows, jnp.clip(c - LAG + 1, 0, rows), rows)
+        return jnp.where(c < LOCAL_STEPS, 0, done)
 
 
     def step(c, carry):
@@ -396,7 +397,7 @@
 
         return carry
 
-    lax.fori_loop(0, rows + LAG + sections - 2, step, 0)
+    lax.fori_loop(0, rows + sections - 1, step, 0)
 
     def drain(k, carry):
         new_write(k).wait()

time: 75 us -> 76.8 us (1.024)
  Pallas kernels: 72.4 us -> 74.2 us
    pallas_call x1, Pallas kernels: 68.4 us -> 70.2 us  [per_device(): pl.pallas_call(functools.partial(exchange_kernel, low, sections), out_sha...]
where the time goes in v7:
time: 76.8 us; the launch traced here: 75.4 us
  Pallas kernels  74.2 us (97%)
  between operations  1.29 us (2%)
    pallas_call x1, Pallas kernels, per_device(): pl.pallas_call(functools.partial(exchange_kernel, low, sections), out_sha...  70.2 us
    pallas_call x1, Pallas kernels, per_device(): pl.pallas_call(results_kernel, out_shape=outs, in_specs=[hbm, hbm], out_s...  2.4 us
    pallas_call x1, Pallas kernels, per_device(): pl.pallas_call(functools.partial(order_kernel, low, rows), out_shape=jax....  1.58 us

profile of v7, /device:TPU:1, one launch (start us, length us, event | category | flops | bytes accessed | tf_op | source)
XLA Modules:
  0.0 75.4 jit_solution(2525496906398316135)
XLA Ops:
  1.3 1.6 %order.1.index = s32[16,128]{1,0:T(8,128)} custom-call(s32[1]{0:T(128)S(6)} %copy.16.ccount, s32[1,128]{1,0:T(1,128)} %bitcast.5, s32[1,128]{1,0:T(1,128)} %bitcast.6, s32[1,128]{1,0:T(1,128)} %bitcast.7, s32[1,128]{1,0:T(1,128)} %bitcast.8, s32[1,128]{1,0:T(1,128)} %bitcast.9), custom_call_target="tpu_custom_call" | custom-call | tf_op jit(solution)/shard_map/order/pallas_call | solution.py:454
  2.9 70.2 %exchange.1 = (f32[16,128,128]{2,1,0:T(8,128)}, f32[16,128,128]{2,1,0:T(8,128)}) custom-call(s32[16,128]{1,0:T(8,128)} %order.1.index, bf16[128,128,128]{2,1,0:T(8,128)(2,1)} %cleft_hbm.1, bf16[128,128,128]{2,1,0:T(8,128)(2,1)} %cright_hbm.1, bf16[16,128,128]{2,1,0:T(8,128)(2,1)} %coup_hbm.1, f32[16,128,128]{2,1,0:T(8,128)} %diag_hbm.1, ...), custom_call_target="tpu_custom_call" | custom-call | tf_op jit(solution)/shard_map/exchange/pallas_call | solution.py:469
  73.0 2.4 %results.1 = (f32[16,128,128]{2,1,0:T(8,128)}, f32[16,128,128]{2,1,0:T(8,128)}) custom-call(f32[16,128,128]{2,1,0:T(8,128)} %get-tuple-element.4.new_in, f32[16,128,128]{2,1,0:T(8,128)} %get-tuple-element.5.adj_in), custom_call_target="tpu_custom_call" | custom-call | tf_op jit(solution)/shard_map/results/pallas_call | solution.py:515
